TPU v7x, 128 devices: a whole 4x4x4 slice. The times are simulated.
128 devices in a mesh: row: 8 (over z, y_lo), col: 16 (over x, y_hi, core).
Axes of the slice: x: 4, y: 4 (y_hi: 2, y_lo: 2; y = y_hi * 2 + y_lo), z: 4, core: 2. Of those that a mesh axis runs over, the one named last changes fastest.
Arguments:
- atom_feat: bfloat16 [16384, 128], P(('row', 'col')), may hold values from -12 to 12
- atom_token: int32 [16384], P(('row', 'col')), may hold values from 0 to 1535, as said below
- window_start: int32 [512], P(('row', 'col')), may hold values from -64 to 16320, as said below
- token_cond: bfloat16 [1536, 768], P('row'), may hold values from -6 to 6
- token_mask: int32 [1536], replicated, may hold values from 0 to 1, as said below
- pair: bfloat16 [1536, 1536, 128], P('row', 'col'), may hold values from -300 to 300
- enc_in: bfloat16 [4, 128, 128], replicated, may hold values from -2 to 2
- enc_out: bfloat16 [128, 128], replicated, may hold values from -0.5 to 0.5
- pool_weight: bfloat16 [128, 768], replicated, may hold values from -0.5 to 0.5
- tok_in: bfloat16 [2, 4, 768, 768], replicated, may hold values from -0.21875 to 0.21875
- tok_out: bfloat16 [2, 768, 768], replicated, may hold values from -0.21875 to 0.21875
- pair_weight: bfloat16 [2, 128, 16], replicated, may hold values from -0.5 to 0.5
- trans_in: bfloat16 [2, 2, 768, 1536], P(None, None, None, 'col'), may hold values from -0.21875 to 0.21875
- trans_out: bfloat16 [2, 1536, 768], P(None, 'col'), may hold values from -0.15625 to 0.15625
- tok_atom: bfloat16 [768, 128], replicated, may hold values from -0.21875 to 0.21875
- dec_in: bfloat16 [4, 128, 128], replicated, may hold values from -2 to 2
- dec_out: bfloat16 [128, 128], replicated, may hold values from -0.5 to 0.5
- pos_out: bfloat16 [3, 128], replicated, may hold values from -0.5 to 0.5
Outputs:
- position_update: float32 [3, 16384], P(None, ('row', 'col'))
Inputs may be any that keep to these rules, and one draw needn't show every extreme that they name: `atom_token`: non-decreasing; every token number 0 to 1535 occurs; for every r, the atoms r * 2048 to (r + 1) * 2048 - 1 belong to the tokens r * 192 to (r + 1) * 192 - 1. window_start[b] lies between 32 b - 64 and 32 b - 32. `token_mask`: ones on a leading run of 768 tokens or more, zeros after, at least one zero.
All inputs are finite; a program needn't handle non-finite values.
Results may differ from a plain program's by a relative error of at most 0.029.
Values may be sent and summed in bfloat16 or wider, within the bound.
A program may use at most 128 MiB of HBM per device.

v0:
```python
import jax
import jax.numpy as jnp
from jax import lax
from jax.sharding import PartitionSpec as P

HA = 4
QB = 32
KW = 128
HALO = 64
BLOCKS = 2


def with_halo(block, sides, width):
    for axis, dim in sides:
        count = lax.axis_size(axis)
        forward = [(i, i + 1) for i in range(count - 1)]
        backward = [(target, source) for source, target in forward]
        low = lax.ppermute(
            lax.slice_in_dim(block, block.shape[dim] - width, None, axis=dim), axis, forward
        )
        high = lax.ppermute(lax.slice_in_dim(block, 0, width, axis=dim), axis, backward)
        block = jnp.concatenate([low, block, high], axis=dim)
    return block


def combined_all(part, axis, combine):
    gathered = jax.tree.map(lambda a: lax.all_gather(a, axis), part)

    def take(source):
        return jax.tree.map(lambda a: lax.dynamic_index_in_dim(a, source, 0, False), gathered)

    return lax.fori_loop(
        1, lax.axis_size(axis), lambda source, state: combine(state, take(source)), take(0)
    )


def normed(x):
    x = x.astype(jnp.float32)
    cent = x - jnp.mean(x, -1, keepdims=True)
    var = jnp.mean(cent * cent, -1, keepdims=True)
    return cent * lax.rsqrt(var + 1e-05)


def atom_layer(x, starts, w_in, w_out):
    rows, width = x.shape
    hsize = width // HA
    nblk = rows // QB
    xn = normed(x).astype(jnp.bfloat16)
    query = jnp.dot(xn, w_in[0], preferred_element_type=jnp.float32).astype(jnp.bfloat16)
    keys = jnp.dot(xn, w_in[1], preferred_element_type=jnp.float32).astype(jnp.bfloat16)
    vals = jnp.dot(xn, w_in[2], preferred_element_type=jnp.float32).astype(jnp.bfloat16)
    gate = jnp.dot(xn, w_in[3], preferred_element_type=jnp.float32)
    both = jnp.concatenate([keys, vals], 1)
    padded = with_halo(both, ((("row", "col"), 0),), HALO)
    natom = lax.axis_size(("row", "col")) * rows
    offset = lax.axis_index(("row", "col")) * rows
    local = starts - offset + HALO
    windows = jax.vmap(lambda s: lax.dynamic_slice_in_dim(padded, s, KW, 0))(local)
    glob = starts[:, None] + jnp.arange(KW, dtype=jnp.int32)[None, :]
    valid = (glob >= 0) & (glob < natom)
    qblk = query.reshape(nblk, QB, HA, hsize)
    kblk = windows[:, :, :width].reshape(nblk, KW, HA, hsize)
    vblk = windows[:, :, width:].reshape(nblk, KW, HA, hsize)
    scores = jnp.einsum(
        "bqhd,bkhd->bhqk", qblk, kblk, preferred_element_type=jnp.float32
    ) / jnp.sqrt(jnp.float32(hsize))
    scores = jnp.where(valid[:, None, None, :], scores, -1000000000.0)
    top = jnp.max(scores, -1, keepdims=True)
    expd = jnp.exp(scores - top)
    total = jnp.sum(expd, -1)
    outs = jnp.einsum(
        "bhqk,bkhd->bqhd", expd.astype(jnp.bfloat16), vblk, preferred_element_type=jnp.float32
    )
    outs = outs / jnp.transpose(total, (0, 2, 1))[:, :, :, None]
    outs = outs.reshape(rows, width)
    gated = (jax.nn.sigmoid(gate) * outs).astype(jnp.bfloat16)
    return (
        x.astype(jnp.float32) + jnp.dot(gated, w_out, preferred_element_type=jnp.float32)
    ).astype(jnp.bfloat16)


def spread_heads(factor, hsize):
    return jnp.repeat(jnp.transpose(factor), hsize, axis=1)


def token_block(act, pair_tile, token_mask, w_in, w_out, w_pair, t_in, t_out):
    rows, width = act.shape
    cols = pair_tile.shape[1]
    heads = w_pair.shape[1]
    hsize = width // heads
    col_start = lax.axis_index("col") * cols
    key_valid = lax.dynamic_slice_in_dim(token_mask, col_start, cols, 0) == 1
    xn = normed(act).astype(jnp.bfloat16)
    query = jnp.dot(xn, w_in[0], preferred_element_type=jnp.float32).astype(jnp.bfloat16)
    gate = jnp.dot(xn, w_in[3], preferred_element_type=jnp.float32)
    keys_own = jnp.dot(xn, w_in[1], preferred_element_type=jnp.float32).astype(jnp.bfloat16)
    vals_own = jnp.dot(xn, w_in[2], preferred_element_type=jnp.float32).astype(jnp.bfloat16)
    whole = lax.all_gather(jnp.concatenate([keys_own, vals_own], 1), "row", axis=0, tiled=True)
    mine = lax.dynamic_slice_in_dim(whole, col_start, cols, 0)
    keys = mine[:, :width]
    vals = mine[:, width:]
    bias = jnp.einsum("qkc,ch->hqk", pair_tile, w_pair, preferred_element_type=jnp.float32)
    qh = query.reshape(rows, heads, hsize)
    kh = keys.reshape(cols, heads, hsize)
    vh = vals.reshape(cols, heads, hsize)
    scores = (
        jnp.einsum("qhd,khd->hqk", qh, kh, preferred_element_type=jnp.float32)
        / jnp.sqrt(jnp.float32(hsize))
        + bias
    )
    scores = jnp.where(key_valid[None, None, :], scores, -1000000000.0)
    top = jnp.max(scores, -1)
    expd = jnp.exp(scores - top[:, :, None])
    total = jnp.sum(expd, -1)
    partial_value = jnp.einsum(
        "hqk,khd->qhd", expd.astype(jnp.bfloat16), vh, preferred_element_type=jnp.float32
    ).reshape(rows, width)

    def combine(first, second):
        joint = jnp.maximum(first[0], second[0])
        scale_one = jnp.exp(first[0] - joint)
        scale_two = jnp.exp(second[0] - joint)
        summed = first[1] * scale_one + second[1] * scale_two
        outs = first[2] * spread_heads(scale_one, hsize) + second[2] * spread_heads(
            scale_two, hsize
        )
        return (joint, summed, outs)

    top, total, partial_value = combined_all((top, total, partial_value), "col", combine)
    attn = partial_value / spread_heads(total, hsize)
    gated = (jax.nn.sigmoid(gate) * attn).astype(jnp.bfloat16)
    act = act + jnp.dot(gated, w_out, preferred_element_type=jnp.float32)
    xn2 = normed(act).astype(jnp.bfloat16)
    swish = jax.nn.silu(jnp.dot(xn2, t_in[0], preferred_element_type=jnp.float32))
    hidden = (swish * jnp.dot(xn2, t_in[1], preferred_element_type=jnp.float32)).astype(
        jnp.bfloat16
    )
    return act + lax.psum(
        jnp.dot(hidden, t_out, preferred_element_type=jnp.float32).astype(jnp.bfloat16), "col"
    ).astype(jnp.float32)


def body(
    atom_feat,
    atom_token,
    window_start,
    token_cond,
    token_mask,
    pair,
    enc_in,
    enc_out,
    pool_weight,
    tok_in,
    tok_out,
    pair_weight,
    trans_in,
    trans_out,
    tok_atom,
    dec_in,
    dec_out,
    pos_out,
):
    row_tokens = token_cond.shape[0]
    row_start = lax.axis_index("row") * row_tokens
    first = atom_layer(atom_feat, window_start, enc_in, enc_out)
    feats = jax.nn.relu(jnp.dot(first, pool_weight, preferred_element_type=jnp.float32)).astype(
        jnp.bfloat16
    )
    local_token = atom_token - row_start
    onehot = local_token[None, :] == jnp.arange(row_tokens, dtype=jnp.int32)[:, None]
    own_sums = jnp.dot(onehot.astype(jnp.bfloat16), feats, preferred_element_type=jnp.float32)
    own_counts = jnp.sum(onehot.astype(jnp.float32), 1)
    sums, counts = (
        lax.psum(own_sums.astype(jnp.bfloat16), "col").astype(jnp.float32),
        lax.psum(own_counts.astype(jnp.bfloat16), "col").astype(jnp.float32),
    )
    act = sums / counts[:, None] + token_cond.astype(jnp.float32)
    for layer in range(BLOCKS):
        act = token_block(
            act,
            pair,
            token_mask,
            tok_in[layer],
            tok_out[layer],
            pair_weight[layer],
            trans_in[layer],
            trans_out[layer],
        )
    proj = jnp.dot(
        normed(act).astype(jnp.bfloat16), tok_atom, preferred_element_type=jnp.float32
    ).astype(jnp.bfloat16)
    spread = jnp.take(proj, local_token, axis=0)
    second = (first.astype(jnp.float32) + spread.astype(jnp.float32)).astype(jnp.bfloat16)
    third = atom_layer(second, window_start, dec_in, dec_out)
    return jnp.dot(
        pos_out,
        jnp.transpose(normed(third).astype(jnp.bfloat16)),
        preferred_element_type=jnp.float32,
    )


def solution(mesh):
    in_specs = (
        P(("row", "col"), None),
        P(("row", "col")),
        P(("row", "col")),
        P("row", None),
        P(),
        P("row", "col", None),
        P(),
        P(),
        P(),
        P(),
        P(),
        P(),
        P(None, None, None, "col"),
        P(None, "col", None),
        P(),
        P(),
        P(),
        P(),
    )
    out_specs = P(None, ("row", "col"))
    return jax.shard_map(body, mesh=mesh, in_specs=in_specs, out_specs=out_specs, check_vma=False)
```

profile of v0, /device:TPU:1, one launch (start us, length us, event | category | flops | bytes accessed | tf_op | source)
XLA Modules:
  0.0 916.4 jit_solution(427668292394923520)
XLA Ops:
  9.6 3.3 collective-permute-start.1
  12.9 4.8 collective-permute-start
  21.6 6.4 while.42
  32.1 33.1 %psum.29 = bf16[192]{0:T(256)(128)(2,1)S(1)} all-reduce(bf16[192]{0:T(256)(128)(2,1)S(1)} %convert_reduce_fusion.1), channel_id=1, replica_groups=mesh['row'=8,'col'=16] {'col'}, use_global_device_ids=true, to_apply=%region_6.7 | all-reduce | flops 192 | bytes 768 | tf_op jit(solution)/shard_map/psum | solution.py:175
  65.2 102.3 %all-reduce.5.cloned.1.call-done = bf16[192,768]{1,0:T(8,128)(2,1)} async-done(((bf16[192,768]{1,0:T(8,128)(2,1)}), bf16[192,768]{1,0:T(8,128)(2,1)}) %all-reduce.5.cloned.1.call-update) | async-done | bytes 294928 | tf_op jit(solution)/shard_map/psum | solution.py:174
  170.0 1.9 convolution_convert_fusion.5
  171.9 1.7 convolution_convert_fusion.6
  174.6 5.3 fusion.168
  182.1 1.9 convolution_convert_fusion.7
  184.9 89.9 %all-gather.9.cloned.1.call-done = bf16[1536,1536]{1,0:T(8,128)(2,1)} async-done(((bf16[192,1536]{1,0:T(8,128)(2,1)}), bf16[1536,1536]{1,0:T(8,128)(2,1)}) %all-gather.9.cloned.1.call-update) | async-done | bytes 4718608 | tf_op jit(solution)/shard_map/all_gather | solution.py:98
  279.3 25.3 %all-gather = f32[256,192]{1,0:T(8,128)S(1)} all-gather(f32[16,192]{1,0:T(8,128)S(1)} %get-tuple-element.509), channel_id=2, replica_groups=mesh['row'=8,'col'=16] {'col'}, dimensions={0}, use_global_device_ids=true | all-gather | bytes 208896 | tf_op jit(solution)/shard_map/all_gather | solution.py:27
  304.8 20.5 %all-gather.1 = f32[256,192]{1,0:T(8,128)S(1)} all-gather(f32[16,192]{1,0:T(8,128)S(1)} %fusion.11), channel_id=3, replica_groups=mesh['row'=8,'col'=16] {'col'}, dimensions={0}, use_global_device_ids=true | all-gather | bytes 208896 | tf_op jit(solution)/shard_map/all_gather | solution.py:27
  325.3 32.8 %all-gather.11.cloned.1.call-done = f32[16,192,768]{2,1,0:T(8,128)} async-done(((f32[1,192,768]{2,1,0:T(8,128)}), f32[16,192,768]{2,1,0:T(8,128)}) %all-gather.11.cloned.1.call-update) | async-done | bytes 9437200 | tf_op jit(solution)/shard_map/all_gather | solution.py:27
  359.5 26.8 %while.40 = (s32[]{:T(128)}, f32[16,192]{1,0:T(8,128)S(1)}, f32[16,192]{1,0:T(8,128)S(1)}, f32[192,768]{0,1:T(8,128)S(1)}, f32[16,16,192]{2,1,0:T(8,128)S(1)}, /...) while((s32[]{:T(128)}, f32[16,192]{1,0:T(8,128)S(1)}, ...), condition=%wide.region_12.13_spmd, body=%wide.region_11.12_spmd.sunk | while | flops 463877 | bytes 4313243 | solution.py:32
  387.4 2.6 fusion.190
  392.5 128.9 %all-reduce.7.cloned.1.call-done = bf16[192,768]{1,0:T(8,128)(2,1)} async-done(((bf16[192,768]{1,0:T(8,128)(2,1)}), bf16[192,768]{1,0:T(8,128)(2,1)}) %all-reduce.7.cloned.1.call-update) | async-done | bytes 294928 | tf_op jit(solution)/shard_map/psum | solution.py:138
  523.9 1.8 convolution_convert_fusion.1
  525.7 1.7 convolution_convert_fusion.2
  528.3 5.3 fusion.166
  533.6 1.9 copy.119
  537.4 91.1 %all-gather.13.cloned.1.call-done = bf16[1536,1536]{1,0:T(8,128)(2,1)} async-done(((bf16[192,1536]{1,0:T(8,128)(2,1)}), bf16[1536,1536]{1,0:T(8,128)(2,1)}) %all-gather.13.cloned.1.call-update) | async-done | bytes 4718608 | tf_op jit(solution)/shard_map/all_gather | solution.py:98
  630.5 2.0 fusion.193
  634.1 25.3 %all-gather.2 = f32[256,192]{1,0:T(8,128)S(1)} all-gather(f32[16,192]{1,0:T(8,128)S(1)} %get-tuple-element.513), channel_id=4, replica_groups=mesh['row'=8,'col'=16] {'col'}, dimensions={0}, use_global_device_ids=true | all-gather | bytes 208896 | tf_op jit(solution)/shard_map/all_gather | solution.py:27
  659.6 21.8 %all-gather.3 = f32[256,192]{1,0:T(8,128)} all-gather(f32[16,192]{1,0:T(8,128)S(1)} %fusion.13), channel_id=5, replica_groups=mesh['row'=8,'col'=16] {'col'}, dimensions={0}, use_global_device_ids=true | all-gather | bytes 208896 | tf_op jit(solution)/shard_map/all_gather | solution.py:27
  682.2 31.0 %all-gather.15.cloned.1.call-done = f32[16,192,768]{2,1,0:T(8,128)} async-done(((f32[1,192,768]{2,1,0:T(8,128)}), f32[16,192,768]{2,1,0:T(8,128)}) %all-gather.15.cloned.1.call-update) | async-done | bytes 9437200 | tf_op jit(solution)/shard_map/all_gather | solution.py:27
  714.6 37.6 %while.41 = (s32[]{:T(128)}, f32[16,192]{1,0:T(8,128)S(1)}, f32[16,192]{1,0:T(8,128)S(1)}, f32[192,768]{0,1:T(8,128)S(1)}, f32[16,16,192]{2,1,0:T(8,128)S(1)}, /...) while((s32[]{:T(128)}, f32[16,192]{1,0:T(8,128)S(1)}, ...), condition=%wide.region_21.22_spmd, body=%wide.region_20.21_spmd.sunk | while | flops 463877 | bytes 4313243 | solution.py:32
  753.1 2.5 fusion.194
  757.2 2.2 convolution_convert_fusion
  759.4 128.8 %all-reduce.9.cloned.1.call-done = bf16[192,768]{1,0:T(8,128)(2,1)} async-done(((bf16[192,768]{1,0:T(8,128)(2,1)}), bf16[192,768]{1,0:T(8,128)(2,1)}) %all-reduce.9.cloned.1.call-update) | async-done | bytes 294928 | tf_op jit(solution)/shard_map/psum | solution.py:138
  892.4 4.1 collective-permute-start.3
  896.4 3.0 collective-permute-start.2
  900.9 5.9 while.43
  (427 shorter events, 123.3 us)
Async XLA Ops:
  6.5 24.2 %copy-start = (bf16[128,768]{1,0:T(8,128)(2,1)S(1)}, bf16[128,768]{1,0:T(8,128)(2,1)}, u32[]{:S(2)}) copy-start(bf16[128,768]{1,0:T(8,128)(2,1)} %param.30) | copy-start | bytes 589828
  6.5 160.9 %all-reduce.5.cloned.1.call-start = ((), (), s32[]{:S(2)}) async-start(), calls=%async_computation | async-start | bytes 589824 | tf_op jit(solution)/shard_map/psum | solution.py:174
  9.6 11.8 %collective-permute-start.1 = (bf16[64,256]{0,1:T(8,128)(2,1)S(1)}, bf16[64,256]{0,1:T(8,128)(2,1)S(1)}, u32[]{:S(2)}, u32[]{:S(2)}) collective-permute-start(bf16[64,256]{0,1:T(8,128)(2,1)S(1)} %get-tuple-element.506), channel_id=1, source_target_pairs={{1,0},{2,1},{3,2},{4,3},{5,4},{6,5},{7,6},{8,7},{9,8},{10,9},{11,1... | collective-permute-start | bytes 98312 | tf_op jit(solution)/shard_map/ppermute | solution.py:21
  12.9 8.5 collective-permute-start
  19.4 9.0 copy-start.24
  20.6 11.3 %copy-start.27 = (s32[128]{0:T(128)}, s32[128]{0:T(128)S(1)}, u32[]{:S(2)}) copy-start(s32[128]{0:T(128)S(1)} %get-tuple-element.490) | copy-start | bytes 1540
  29.0 138.5 %copy-start.4 = (bf16[192,768]{1,0:T(8,128)(2,1)S(1)}, bf16[192,768]{1,0:T(8,128)(2,1)}, u32[]{:S(2)}) copy-start(bf16[192,768]{1,0:T(8,128)(2,1)} %param.25) | copy-start | bytes 884740
  30.7 141.2 %copy-start.13 = (bf16[128,128]{0,1:T(8,128)(2,1)}, bf16[128,128]{0,1:T(8,128)(2,1)S(1)}, u32[]{:S(2)}) copy-start(bf16[128,128]{0,1:T(8,128)(2,1)S(1)} %fusion.60) | copy-start | bytes 98308
  31.9 242.9 %all-gather.9.cloned.1.call-start = ((), (), s32[]{:S(2)}) async-start(), calls=%async_computation.1 | async-start | bytes 5308416 | tf_op jit(solution)/shard_map/all_gather | solution.py:98
  65.2 116.9 %copy-start.20 = (f32[192]{0:T(256)}, f32[192]{0:T(256)S(1)}, u32[]{:S(2)}) copy-start(f32[192]{0:T(256)S(1)} %convert_element_type.167) | copy-start | bytes 2308
  168.7 13.4 %copy-start.22 = (f32[192]{0:T(256)}, f32[192]{0:T(256)S(1)}, u32[]{:S(2)}) copy-start(f32[192]{0:T(256)S(1)} %broadcast_multiply_fusion.4) | copy-start | bytes 2308
  170.0 12.1 %copy-start.31 = (f32[192]{0:T(256)}, f32[192]{0:T(256)S(1)}, u32[]{:S(2)}) copy-start(f32[192]{0:T(256)S(1)} %add_rsqrt_fusion.4) | copy-start | bytes 2308
  174.5 183.5 %all-gather.11.cloned.1.call-start = ((), (), s32[]{:S(2)}) async-start(), calls=%async_computation.2 | async-start | bytes 10027008 | tf_op jit(solution)/shard_map/all_gather | solution.py:27
  279.2 242.1 %all-reduce.7.cloned.1.call-start = ((), (), s32[]{:S(2)}) async-start(), calls=%async_computation.3 | async-start | bytes 589824 | tf_op jit(solution)/shard_map/psum | solution.py:138
  387.4 3.0 copy-start.12
  392.2 236.3 %all-gather.13.cloned.1.call-start = ((), (), s32[]{:S(2)}) async-start(), calls=%async_computation.4 | async-start | bytes 5308416 | tf_op jit(solution)/shard_map/all_gather | solution.py:98
  521.3 2.4 copy-start.2
  523.9 11.7 %copy-start.9 = (bf16[192,768]{1,0:T(8,128)(2,1)}, bf16[192,768]{1,0:T(8,128)(2,1)S(1)}, u32[]{:S(2)}) copy-start(bf16[192,768]{1,0:T(8,128)(2,1)S(1)} %multiply_convert_fusion.2) | copy-start | bytes 884740
  525.7 2.6 copy-start.19
  528.2 184.9 %all-gather.15.cloned.1.call-start = ((), (), s32[]{:S(2)}) async-start(), calls=%async_computation.5 | async-start | bytes 10027008 | tf_op jit(solution)/shard_map/all_gather | solution.py:27
  535.5 95.0 %copy-start.29 = (pred[96]{0:T(512)(128)(4,1)S(1)}, pred[96]{0:T(512)(128)(4,1)}, u32[]{:S(2)}) copy-start(pred[96]{0:T(512)(128)(4,1)} %dynamic-slice_compare_fusion) | copy-start | bytes 292
  634.0 254.2 %all-reduce.9.cloned.1.call-start = ((), (), s32[]{:S(2)}) async-start(), calls=%async_computation.6 | async-start | bytes 589824 | tf_op jit(solution)/shard_map/psum | solution.py:138
  755.8 3.5 copy-start.28
  757.1 133.4 %copy-start.11 = (bf16[768,128]{1,0:T(8,128)(2,1)S(1)}, bf16[768,128]{1,0:T(8,128)(2,1)}, u32[]{:S(2)}) copy-start(bf16[768,128]{1,0:T(8,128)(2,1)} %param.36) | copy-start | bytes 589828
  759.4 132.3 %copy-start.14 = (bf16[128,128]{0,1:T(8,128)(2,1)S(1)}, bf16[128,128]{0,1:T(8,128)(2,1)}, u32[]{:S(2)}) copy-start(bf16[128,128]{0,1:T(8,128)(2,1)} %copy-done.13) | copy-start | bytes 98308
  759.4 132.3 %copy-start.26 = (pred[128]{0:T(512)(128)(4,1)S(1)}, pred[128]{0:T(512)(128)(4,1)}, u32[]{:S(2)}) copy-start(pred[128]{0:T(512)(128)(4,1)} %get-tuple-element.489) | copy-start | bytes 388
  759.4 132.4 %copy-start.17 = (bf16[4,128,128]{2,1,0:T(8,128)(2,1)S(1)}, bf16[4,128,128]{2,1,0:T(8,128)(2,1)}, u32[]{:S(2)}) copy-start(bf16[4,128,128]{2,1,0:T(8,128)(2,1)} %param.37) | copy-start | bytes 393220
  888.2 2.4 copy-start.3
  890.5 10.4 %copy-start.16 = (s32[4,2]{0,1:T(2,128)S(1)}, s32[4,2]{0,1:T(2,128)}, u32[]{:S(2)}) copy-start(s32[4,2]{0,1:T(2,128)} %copy-done.15) | copy-start | bytes 100
  892.4 7.4 collective-permute-start.3
  896.4 4.3 collective-permute-start.2
  900.9 6.3 copy-start.25
  (16 other events, 21.0 us)
Sparse Core Ops, SparseCore 0:
  32.0 135.3 all-reduce.4
  174.7 100.1 all-gather.8
  279.3 78.7 all-gather.10
  392.4 128.9 all-reduce.6
  528.4 100.1 all-gather.12
  634.1 79.0 all-gather.14
  759.5 128.6 all-reduce.8
where the time goes:
time: 926 us; the launch traced here: 916 us
  waiting for transfers between devices  606 us (65%)
  blocking collectives  126 us (14%)
  local copies, waits for them, and re-layouts  71.7 us (8%)
  matrix products  43.7 us (5%)
  other arithmetic  37.1 us (4%)
  starting transfers between devices  15.6 us (2%)
  between operations  14.5 us (2%)
    psum x2, waiting for transfers between devices, token_block(): lax.psum(jnp.dot(hidden, t_out, preferred_element_type=jnp.float32).astyp...  258 us
    all_gather x2, waiting for transfers between devices, token_block(): lax.all_gather(jnp.concatenate([keys_own, vals_own], 1), 'row', axis=0, t...  181 us
    psum x1, waiting for transfers between devices, body(): lax.psum(own_sums.astype(jnp.bfloat16), 'col').astype(jnp.float32)  102 us
    all_gather x4, blocking collectives, combined_all(): gathered = jax.tree.map(lambda a: lax.all_gather(a, axis), part)  92.9 us
    all_gather x2, waiting for transfers between devices, combined_all(): gathered = jax.tree.map(lambda a: lax.all_gather(a, axis), part)  63.8 us
    dynamic_slice x64, local copies, waits for them, and re-layouts, take(): lax.dynamic_index_in_dim(a, source, 0, False)  41.9 us
    psum x1, blocking collectives, body(): lax.psum(own_counts.astype(jnp.bfloat16), 'col').astype(jnp.float32)  33.1 us
  transfers between devices with their start and end apart: 11, of which 8 were waited for; matrix products, arithmetic and copies ran while one was open for 3% of the time, Pallas kernels for 0%

commit v1 on v0

v1 whole, which is shorter than its diff:
```python
import math

import jax
import jax.numpy as jnp
from jax import lax
from jax.experimental import pallas as pl
from jax.experimental.pallas import tpu as pltpu
from jax.sharding import PartitionSpec as P

MESH = pl.DeviceIdType.MESH
F32 = jnp.float32
BF16 = jnp.bfloat16
NEG = -1000000000.0
NR = 8
NC = 16
NCH = 8
OWN = 6
QT = 96


def dot(a, b):
    return jnp.dot(a, b, preferred_element_type=F32)


def dot_t(a, b):
    return lax.dot_general(a, b, (((1,), (1,)), ((), ())), preferred_element_type=F32)


def normed(x):
    cent = x - jnp.mean(x, -1, keepdims=True)
    var = jnp.mean(cent * cent, -1, keepdims=True)
    return cent * lax.rsqrt(var + 1e-05)


def iota(shape, dim):
    return lax.broadcasted_iota(jnp.int32, shape, dim)


def atom_layer(xf, valid, w_in, w_out):
    n = normed(xf).astype(BF16)
    own = n[:128]
    q = dot(own, w_in[0]).astype(BF16).astype(F32)
    keys = dot(n, w_in[1]).astype(BF16)
    vals = dot(n, w_in[2]).astype(BF16)
    gate = dot(own, w_in[3])
    head = iota((128, 128), 1) // 32
    outs = jnp.zeros((128, 128), F32)
    for h in range(4):
        qh = jnp.where(head == h, q, 0.0).astype(BF16)
        s = dot_t(qh, keys) * (1.0 / math.sqrt(32.0))
        s = jnp.where(valid, s, NEG)
        e = jnp.exp(s - jnp.max(s, -1, keepdims=True))
        total = jnp.sum(e, -1, keepdims=True)
        o = dot(e.astype(BF16), vals) / total
        outs = jnp.where(head == h, o, outs)
    gated = (jax.nn.sigmoid(gate) * outs).astype(BF16)
    return (xf[:128] + dot(gated, w_out[...])).astype(BF16)


def kernel(
    ws,
    tok,
    mask,
    x_in,
    wt,
    cond_h,
    pair_h,
    enc_in_h,
    enc_out_h,
    pool_h,
    tok_in_h,
    tok_out_h,
    tin_h,
    tout_h,
    tok_atom_h,
    dec_in_h,
    dec_out_h,
    pos_h,
    out,
    cond,
    pair,
    enc_in,
    enc_out,
    pool,
    slab,
    wq,
    topad,
    tin,
    tout,
    tok_atom,
    dec_in,
    dec_out,
    pos,
    xh,
    x1all,
    xe,
    zb,
    bb,
    kv,
    ssc,
    ob,
    prt,
    rsb,
    db,
    act,
    acc,
    proj,
    lsem,
    h_ss,
    h_rs,
    x_ss,
    x_rs,
    e_ss,
    e_rs,
    t_ss,
    t_rs,
    b_ss,
    b_rs,
    kv_ss,
    kv_rs,
    o_ss,
    o_rs,
    r_ss,
    r_rs,
    d_ss,
    d_rs,
    p_ss,
    p_rs,
):
    r = lax.axis_index("row")
    c = lax.axis_index("col")
    i = c // 2
    k = c % 2
    sib = (r, c + 1 - 2 * k)
    flat = r * NC + c
    nxt = (flat + 1) % (NR * NC)
    prv = (flat + NR * NC - 1) % (NR * NC)
    nxt = (nxt // NC, nxt % NC)
    prv = (prv // NC, prv % NC)
    is_owner = i < OWN
    is_tail = jnp.logical_and(k == 1, jnp.logical_and(i >= 2, i < OWN))
    is_head = jnp.logical_and(k == 0, i < 4)

    def chip(j):
        return (r, 2 * ((i + j) % NCH) + k)

    def rcopy(src, dst, ss, rs, dev):
        return pltpu.make_async_remote_copy(
            src_ref=src, dst_ref=dst, send_sem=ss, recv_sem=rs, device_id=dev, device_id_type=MESH
        )

    nload = [0]

    def load(src, dst):
        cp = pltpu.make_async_copy(src, dst, lsem.at[nload[0]])
        nload[0] += 1
        cp.start()
        return cp

    ld_pair = [load(pair_h.at[48 * j : 48 * j + 48], pair.at[48 * j : 48 * j + 48]) for j in range(4)]
    ld_enc = [load(enc_in_h, enc_in), load(enc_out_h, enc_out)]
    ld_pool = [
        load(pool_h, pool),
        load(cond_h.at[pl.ds(pl.multiple_of(QT * k, 32), QT)], cond),
    ]
    base = jnp.minimum(128 * ((QT * i) // 128), 512)
    base = pl.multiple_of(base, 128)
    shift = QT * i - base
    ld_slab = [load(tok_in_h.at[:, :, pl.ds(base, 256)], slab)]
    ld_tok = [
        load(tok_out_h, topad.at[:, 0:QT]),
        load(tin_h, tin.at[k]),
        load(tout_h, tout.at[k]),
        load(tok_atom_h, tok_atom),
        load(dec_in_h, dec_in),
        load(dec_out_h, dec_out),
        load(pos_h, pos),
    ]

    topad[:, QT:, :] = jnp.zeros((16, 32, 768), BF16)
    kv[:, :, :, QT:, :] = jnp.zeros((2, 16, 2, 32, 128), BF16)
    proj[...] = jnp.zeros((384, 128), BF16)

    bar = pltpu.get_barrier_semaphore()

    def greet(dev):
        pl.semaphore_signal(bar, inc=1, device_id=dev, device_id_type=MESH)

    for j in range(1, NC):
        greet((r, (c + j) % NC))
    for j in range(1, NR):
        greet(((r + j) % NR, c))
    greet(nxt)
    greet(prv)

    @pl.when(c == 0)
    def _():
        for o in (5, 7, 9, 11):
            greet(((r + NR - 1) % NR, o))

    @pl.when(c == NC - 1)
    def _():
        for o in (0, 2, 4, 6):
            greet(((r + 1) % NR, o))

    extra = jnp.where(jnp.logical_or(is_tail, is_head), 1, 0)
    pl.semaphore_wait(bar, 24 + extra)

    halo = [
        rcopy(x_in.at[64:128], xh.at[1], h_ss.at[0], h_rs.at[1], nxt),
        rcopy(x_in.at[0:64], xh.at[0], h_ss.at[1], h_rs.at[0], prv),
    ]
    for cp in halo:
        cp.start()
    swap = [
        rcopy(tin_h, tin.at[k], t_ss.at[0], t_rs.at[0], sib),
        rcopy(tout_h, tout.at[k], t_ss.at[1], t_rs.at[1], sib),
    ]
    for cp in swap:
        cp.start()

    def bias_half(kp):
        w = wt[...]
        for kb in range(3):

            @pl.loop(0, 12)
            def _(u):
                t = 24 * kb + 2 * u
                rows = []
                for d in range(2):
                    rows.append(pair[QT * kp + t + d])
                    rows.append(pair[QT * kp + 72 + 2 * u + d, 32 * kb : 32 * kb + 32, :])
                res = dot_t(w, jnp.concatenate(rows, 0))
                zf = zb.reshape(32 * 144, 128)
                for d in range(2):
                    for g in range(4):
                        zf[pl.ds(g * 8 * 144 + kp * 72 + t + d, 8, stride=144), :] = res[
                            8 * g : 8 * g + 8, 128 * d : 128 * d + 128
                        ]

    def bias_src(b, dev):
        return zb.at[
            pl.ds(16 * b + 2 * (dev // 2), 2), pl.ds(pl.multiple_of(72 * (dev % 2), 8), 72), :
        ]

    def bias_send(b, j):
        dev = (c + j) % NC
        return rcopy(bias_src(b, dev), bb.at[b, c], b_ss.at[b, j], b_rs.at[b, c], (r, dev))

    ld_pair[0].wait()
    ld_pair[1].wait()
    bias_half(0)

    for cp in ld_enc:
        cp.wait()
    for cp in halo:
        cp.wait_recv()
    rowi = iota((128, 256), 0)
    coli = iota((128, 256), 1)
    glob = flat * 128 + jnp.where(coli < 192, coli, coli - 256)
    start = jnp.where(
        rowi < 64, jnp.where(rowi < 32, ws[0], ws[1]), jnp.where(rowi < 96, ws[2], ws[3])
    )
    start = jnp.maximum(start, 0)
    stop = jnp.where(
        rowi < 64, jnp.where(rowi < 32, ws[0], ws[1]), jnp.where(rowi < 96, ws[2], ws[3])
    ) + 128
    stop = jnp.minimum(stop, NR * NC * 128)
    valid = jnp.logical_and(glob >= start, glob < stop)
    xf = jnp.concatenate([x_in[...], xh[0], xh[1]], 0).astype(F32)
    x1 = atom_layer(xf, valid, enc_in, enc_out)
    tokrow = (tok[...] - 192 * r).astype(F32)
    tokrows = jnp.broadcast_to(tokrow, (16, 128)).astype(BF16)
    x1all[c, 0:16, :] = tokrows
    x1all[c, 16:144, :] = x1
    x1all[c, 144:160, :] = tokrows

    edge = [
        rcopy(x1all.at[c, 80:160], xe.at[1], e_ss.at[0], e_rs.at[1], nxt),
        rcopy(x1all.at[c, 0:80], xe.at[0], e_ss.at[1], e_rs.at[0], prv),
    ]

    def x1_slot(s):
        return x1all.at[s, 0:144]

    x_send = [
        rcopy(x1_slot(c), x1_slot(c), x_ss.at[j], x_rs.at[c], chip(j)) for j in range(1, NCH)
    ]
    x_fwd = []
    for j in range(NCH):
        s = 2 * ((i + j) % NCH) + k
        x_fwd.append(rcopy(x1_slot(s), x1_slot(s), x_ss.at[NCH + j], x_rs.at[s], sib))
    x_far = []
    for j in range(NCH):
        s = 2 * ((i + j) % NCH) + 1 - k
        x_far.append(rcopy(x1_slot(s), x1_slot(s), x_ss.at[NCH + j], x_rs.at[s], sib))
    for cp in x_send:
        cp.start()
    x_fwd[0].start()
    for cp in edge:
        cp.start()

    ld_pair[2].wait()
    ld_pair[3].wait()
    bias_half(1)
    b_send = [[bias_send(b, j) for j in range(1, NC)] for b in range(2)]
    b_own = []
    for b in range(2):
        cp = pltpu.make_async_copy(bias_src(b, c), bb.at[b, c], lsem.at[nload[0] + b])
        cp.start()
        b_own.append(cp)
    for cp in b_send[0]:
        cp.start()

    for cp in ld_slab:
        cp.wait()
    pick = jnp.logical_and(
        iota((256, 128), 0) == iota((256, 128), 1) + shift, iota((256, 128), 1) < QT
    )
    pick = jnp.where(pick, 1.0, 0.0).astype(BF16)

    @pl.loop(0, 8)
    def _(m):
        wq[m] = dot(slab[m], pick).astype(BF16)

    for j in range(1, NCH):
        s = 2 * ((i + j) % NCH) + k
        rcopy(x1_slot(s), x1_slot(s), x_ss.at[0], x_rs.at[s], sib).wait_recv()
        x_fwd[j].start()
    for cp in x_far:
        cp.wait_recv()
    for cp in ld_pool:
        cp.wait()
    acc[...] = jnp.zeros((QT, 768), F32)

    def pool_step(s2, cnt):
        both = jnp.concatenate([x1all[2 * s2, 16:144, :], x1all[2 * s2 + 1, 16:144, :]], 0)
        feats = jnp.maximum(dot(both, pool[...]), 0.0).astype(BF16)
        hots = []
        want = (iota((QT, 128), 0) + QT * k).astype(F32)
        for d in range(2):
            t = x1all[2 * s2 + d, 0:16, :].astype(F32)[0:1]
            hots.append(jnp.where(t == want, 1.0, 0.0))
        acc[...] += dot(jnp.concatenate(hots, 1).astype(BF16), feats)
        return cnt + hots[0] + hots[1]

    cnt = lax.fori_loop(0, 8, pool_step, jnp.zeros((QT, 128), F32))
    act[...] = acc[...] / jnp.sum(cnt, -1, keepdims=True) + cond[...].astype(F32)

    nvalid = jnp.sum(
        jnp.sum(mask[...].astype(F32), 1, keepdims=True), 0, keepdims=True
    )
    lane = iota((1, 128), 1)
    lanef = lane.astype(F32)
    mine = 2 * r + k

    def kv_slot(b, s):
        return kv.at[b, s, :, 0:QT, :]

    pend = []
    for b in range(2):
        n = normed(act[...]).astype(BF16)
        kv[b, mine, 0, 0:QT, :] = dot(n, wq[4 * b + 1]).astype(BF16)
        kv[b, mine, 1, 0:QT, :] = dot(n, wq[4 * b + 2]).astype(BF16)
        for j in range(1, NR):
            cp = rcopy(
                kv_slot(b, mine),
                kv_slot(b, mine),
                kv_ss.at[b, j],
                kv_rs.at[b, mine],
                ((r + j) % NR, c),
            )
            cp.start()
            pend.append(cp)
        fwd = []
        for j in range(NR):
            s = 2 * ((r + j) % NR) + k
            fwd.append(
                rcopy(kv_slot(b, s), kv_slot(b, s), kv_ss.at[b, NR + j], kv_rs.at[b, s], sib)
            )
        fwd[0].start()
        pend += fwd
        q = dot(n, wq[4 * b]).astype(BF16).astype(F32)
        gate = dot(n, wq[4 * b + 3])
        lq = iota((QT, 128), 1)
        qs = jnp.concatenate(
            [
                jnp.where(lq < 48, q, 0.0),
                jnp.where(lq < 48, 0.0, q),
            ],
            0,
        ).astype(BF16)
        b_own[b].wait()
        for j in range(1, NC):
            s = (c + j) % NC
            rcopy(bb.at[b, s], bb.at[b, s], b_ss.at[b, 0], b_rs.at[b, s], sib).wait_recv()
        for j in range(1, NR):
            s = 2 * ((r + j) % NR) + k
            rcopy(kv_slot(b, s), kv_slot(b, s), kv_ss.at[b, 0], kv_rs.at[b, s], sib).wait_recv()
            fwd[j].start()
        for j in range(NR):
            s = 2 * ((r + j) % NR) + 1 - k
            rcopy(kv_slot(b, s), kv_slot(b, s), kv_ss.at[b, 0], kv_rs.at[b, s], sib).wait_recv()
        if b == 0:
            for cp in b_send[1]:
                cp.start()

        def score_step(s2, mx):
            keys = jnp.concatenate([kv[b, 2 * s2, 0], kv[b, 2 * s2 + 1, 0]], 0)
            s = dot_t(qs, keys) * (1.0 / math.sqrt(48.0))
            for d in range(2):
                slot = 2 * s2 + d
                first = (QT * slot).astype(F32)
                ok = lanef + first < jnp.minimum(nvalid, first + QT)
                parts = []
                for h in range(2):
                    m = bb[b, slot, h]
                    tail = jnp.where(
                        lane < 32,
                        pltpu.roll(m[0:24], 32, 1),
                        jnp.where(
                            lane < 64, pltpu.roll(m[24:48], 64, 1), pltpu.roll(m[48:72], 96, 1)
                        ),
                    )
                    parts += [m, tail]
                sc = jnp.where(ok, s[:, 128 * d : 128 * d + 128] + jnp.concatenate(parts, 0), NEG)
                ssc[slot] = sc
                mx = jnp.maximum(mx, sc)
            return mx

        mx = lax.fori_loop(0, 8, score_step, jnp.full((2 * QT, 128), 2 * NEG, F32))
        top = jnp.max(mx, -1, keepdims=True)

        def value_step(s2, state):
            tot, o = state
            e0 = jnp.exp(ssc[2 * s2] - top)
            e1 = jnp.exp(ssc[2 * s2 + 1] - top)
            p = jnp.concatenate([e0, e1], 1).astype(BF16)
            vals = jnp.concatenate([kv[b, 2 * s2, 1], kv[b, 2 * s2 + 1, 1]], 0)
            return tot + (e0 + e1), o + dot(p, vals)

        zero = jnp.zeros((2 * QT, 128), F32)
        tot, o = lax.fori_loop(0, 8, value_step, (zero, zero))
        o = o / jnp.sum(tot, -1, keepdims=True)
        o = jnp.where(lq < 48, o[:QT], o[QT:])
        ob[b, i] = (jax.nn.sigmoid(gate) * o).astype(BF16)
        for j in range(1, NCH):
            cp = rcopy(ob.at[b, i], ob.at[b, i], o_ss.at[b, j], o_rs.at[b, i], chip(j))
            cp.start()
            pend.append(cp)
        if b == 0:
            for cp in ld_tok:
                cp.wait()
            for cp in swap:
                cp.wait_recv()
        for j in range(1, NCH):
            s = (i + j) % NCH
            rcopy(ob.at[b, s], ob.at[b, s], o_ss.at[b, 0], o_rs.at[b, s], sib).wait_recv()
        gated = jnp.concatenate([ob[b, s] for s in range(NCH)], 1)
        act[...] += dot(gated, topad[8 * b : 8 * b + 8].reshape(1024, 768))

        m = normed(act[...]).astype(BF16)
        part = jnp.zeros((QT, 768), F32)
        for s in range(2):
            swish = jax.nn.silu(dot(m, tin[s, b, 0]))
            hidden = (swish * dot(m, tin[s, b, 1])).astype(BF16)
            part = part + dot(hidden, tout[s, b])
        prt[b] = part.astype(BF16)
        for o_ in range(OWN):

            @pl.when(i != o_)
            def _():
                rcopy(
                    prt.at[b, 16 * o_ : 16 * o_ + 16],
                    rsb.at[b, i],
                    r_ss.at[b, o_],
                    r_rs.at[b, i],
                    (r, 2 * o_ + k),
                ).start()

        @pl.when(is_owner)
        def _():
            row0 = pl.multiple_of(16 * i, 16)
            rsb[b, i] = prt[b, pl.ds(row0, 16), :]
            for j in range(1, NCH):
                s = (i + j) % NCH
                rcopy(rsb.at[b, s], rsb.at[b, s], r_ss.at[b, 0], r_rs.at[b, s], sib).wait_recv()
            total = rsb[b, 0].astype(F32)
            for s in range(1, NCH):
                total = total + rsb[b, s].astype(F32)
            if b == 0:
                db[i] = total.astype(BF16)
                for j in range(1, NCH):
                    rcopy(db.at[i], db.at[i], d_ss.at[j], d_rs.at[i], chip(j)).start()
            else:
                last = act[pl.ds(row0, 16), :] + total
                here = pl.multiple_of(64 + QT * k + 16 * i, 16)
                mine_p = proj.at[pl.ds(here, 16)]
                proj[pl.ds(here, 16), :] = dot(
                    normed(last).astype(BF16), tok_atom[...]
                ).astype(BF16)
                for j in range(1, NC):
                    rcopy(
                        mine_p, mine_p, p_ss.at[j], p_rs.at[OWN * k + i], (r, (c + j) % NC)
                    ).start()

                @pl.when(is_tail)
                def _():
                    rcopy(
                        mine_p,
                        proj.at[pl.ds(pl.multiple_of(16 * (i - 2), 16), 16)],
                        p_ss.at[16],
                        p_rs.at[10 + i],
                        ((r + 1) % NR, 0),
                    ).start()

                @pl.when(is_head)
                def _():
                    rcopy(
                        mine_p,
                        proj.at[pl.ds(pl.multiple_of(256 + 16 * i, 16), 16)],
                        p_ss.at[16],
                        p_rs.at[12 + i],
                        ((r + NR - 1) % NR, NC - 1),
                    ).start()

        if b == 0:
            for o_ in range(OWN):

                @pl.when(i != o_)
                def _():
                    rcopy(db.at[o_], db.at[o_], d_ss.at[0], d_rs.at[o_], sib).wait_recv()

            act[...] += jnp.concatenate([db[s].astype(F32) for s in range(OWN)], 0)

    for cp in edge:
        cp.wait_recv()
    half = iota((1, 128), 1) < 64
    high = xe[0, 0:16, :].astype(F32)[0:1] + jnp.where(c == NC - 1, 192.0, 0.0)
    low = xe[1, 64:80, :].astype(F32)[0:1] - jnp.where(c == 0, 192.0, 0.0)
    side = jnp.where(half, high, low) + 64.0
    tcol = jnp.concatenate(
        [
            jnp.transpose(jnp.broadcast_to(tokrow + 64.0, (128, 128))),
            jnp.transpose(jnp.broadcast_to(side, (128, 128))),
        ],
        0,
    )
    lane2 = iota((256, 128), 1).astype(F32)
    hot = jnp.concatenate(
        [jnp.where(tcol == lane2 + 128.0 * t, 1.0, 0.0) for t in range(3)], 1
    ).astype(BF16)
    x1cat = jnp.concatenate([x1all[c, 16:144, :], xe[0, 16:80, :], xe[1, 0:64, :]], 0).astype(F32)

    def proj_wait(slot, row, n):
        ref = proj.at[row : row + n]
        rcopy(ref, ref, p_ss.at[0], p_rs.at[slot], sib).wait_recv()

    for s in range(2 * OWN):

        @pl.when(jnp.logical_or(i >= OWN, s != OWN * k + i))
        def _():
            proj_wait(s, 64 + 16 * s, 16)

    @pl.when(c == 0)
    def _():
        for s in range(4):
            proj_wait(12 + s, 16 * s, 16)

    @pl.when(c == NC - 1)
    def _():
        for s in range(4):
            proj_wait(12 + s, 256 + 16 * s, 16)

    spread = dot(hot, proj[...])
    x2 = (x1cat + spread).astype(BF16).astype(F32)
    x3 = atom_layer(x2, valid, dec_in, dec_out)
    n3 = normed(x3.astype(F32)).astype(BF16)
    out[...] = dot_t(pos[...], n3)

    for cp in halo + swap + edge + x_send + x_fwd + b_send[0] + b_send[1] + pend:
        cp.wait_send()
    for b in range(2):
        for o_ in range(OWN):

            @pl.when(i != o_)
            def _():
                src = prt.at[b, 16 * o_ : 16 * o_ + 16]
                rcopy(src, rsb.at[b, i], r_ss.at[b, o_], r_rs.at[b, i], sib).wait_send()

    @pl.when(is_owner)
    def _():
        for j in range(1, NCH):
            rcopy(db.at[i], db.at[i], d_ss.at[j], d_rs.at[i], sib).wait_send()
        ref = proj.at[pl.ds(pl.multiple_of(64 + QT * k + 16 * i, 16), 16)]
        for j in range(1, NC):
            rcopy(ref, ref, p_ss.at[j], p_rs.at[0], sib).wait_send()

        @pl.when(jnp.logical_or(is_tail, is_head))
        def _():
            rcopy(ref, ref, p_ss.at[16], p_rs.at[0], sib).wait_send()


def body(
    atom_feat,
    atom_token,
    window_start,
    token_cond,
    token_mask,
    pair,
    enc_in,
    enc_out,
    pool_weight,
    tok_in,
    tok_out,
    pair_weight,
    trans_in,
    trans_out,
    tok_atom,
    dec_in,
    dec_out,
    pos_out,
):
    vm = pl.BlockSpec(memory_space=pltpu.VMEM)
    hb = pl.BlockSpec(memory_space=pl.ANY)
    dma = pltpu.SemaphoreType.DMA
    wt = jnp.transpose(pair_weight, (0, 2, 1)).reshape(32, 128)
    V = pltpu.VMEM
    scratch = [
        V((QT, 768), BF16),
        V((192, 96, 128), BF16),
        V((4, 128, 128), BF16),
        V((128, 128), BF16),
        V((128, 768), BF16),
        V((8, 768, 256), BF16),
        V((8, 768, 128), BF16),
        V((16, 128, 768), BF16),
        V((2, 2, 2, 768, 96), BF16),
        V((2, 2, 96, 768), BF16),
        V((768, 128), BF16),
        V((4, 128, 128), BF16),
        V((128, 128), BF16),
        V((3, 128), BF16),
        V((2, 64, 128), BF16),
        V((16, 160, 128), BF16),
        V((2, 80, 128), BF16),
        V((32, 144, 128), F32),
        V((2, 16, 2, 72, 128), F32),
        V((2, 16, 2, 128, 128), BF16),
        V((16, 192, 128), F32),
        V((2, 8, QT, 128), BF16),
        V((2, QT, 768), BF16),
        V((2, 8, 16, 768), BF16),
        V((6, 16, 768), BF16),
        V((QT, 768), F32),
        V((QT, 768), F32),
        V((384, 128), BF16),
        dma((24,)),
        dma((2,)),
        dma((2,)),
        dma((16,)),
        dma((16,)),
        dma((2,)),
        dma((2,)),
        dma((2,)),
        dma((2,)),
        dma((2, 16)),
        dma((2, 16)),
        dma((2, 16)),
        dma((2, 16)),
        dma((2, 8)),
        dma((2, 8)),
        dma((2, 8)),
        dma((2, 8)),
        dma((8,)),
        dma((8,)),
        dma((17,)),
        dma((16,)),
    ]
    return pl.pallas_call(
        kernel,
        out_shape=jax.ShapeDtypeStruct((3, 128), F32),
        in_specs=[pl.BlockSpec(memory_space=pltpu.SMEM)] + [vm] * 4 + [hb] * 13,
        out_specs=vm,
        scratch_shapes=scratch,
        compiler_params=pltpu.CompilerParams(
            collective_id=0, has_side_effects=True, vmem_limit_bytes=56 << 20
        ),
        name="diffusion_step",
    )(
        window_start,
        atom_token.reshape(1, 128),
        token_mask.reshape(12, 128),
        atom_feat,
        wt,
        token_cond,
        pair,
        enc_in,
        enc_out,
        pool_weight,
        tok_in.reshape(8, 768, 768),
        tok_out.reshape(16, 96, 768),
        trans_in,
        trans_out,
        tok_atom,
        dec_in,
        dec_out,
        pos_out,
    )


def solution(mesh):
    in_specs = (
        P(("row", "col"), None),
        P(("row", "col")),
        P(("row", "col")),
        P("row", None),
        P(),
        P("row", "col", None),
        P(),
        P(),
        P(),
        P(),
        P(),
        P(),
        P(None, None, None, "col"),
        P(None, "col", None),
        P(),
        P(),
        P(),
        P(),
    )
    out_specs = P(None, ("row", "col"))
    return jax.shard_map(body, mesh=mesh, in_specs=in_specs, out_specs=out_specs, check_vma=False)
```

time: 926 us -> 114 us (0.12)
  waiting for transfers between devices: 606 us -> 0 us
  blocking collectives: 126 us -> 0 us
  Pallas kernels: 0 us -> 110 us
  local copies, waits for them, and re-layouts: 71.7 us -> 3.47 us
  matrix products: 43.7 us -> 0 us
  other arithmetic: 37.1 us -> 0 us
  starting transfers between devices: 15.6 us -> 0 us
  between operations: 14.5 us -> 0.01 us
    psum x3 -> x0, waiting for transfers between devices: 360 us -> none  [the longest x2 258 us: token_block(): lax.psum(jnp.dot(hidden, t_out, preferred_element_type=jnp.float32).astyp...]
    all_gather x4 -> x0, waiting for transfers between devices: 245 us -> none  [the longest x2 181 us: token_block(): lax.all_gather(jnp.concatenate([keys_own, vals_own], 1), 'row', axis=0, t...]
    pallas_call x0 -> x1, Pallas kernels: none -> 110 us  [body(): pl.pallas_call(kernel, out_shape=jax.ShapeDtypeStruct((3, 128), F32), in_...]
    all_gather x4 -> x0, blocking collectives: 92.9 us -> none  [combined_all(): gathered = jax.tree.map(lambda a: lax.all_gather(a, axis), part)]
    dot_general x33 -> x0, matrix products: 43.7 us -> none  [the longest x2 10.6 us: token_block(): jnp.einsum('qkc,ch->hqk', pair_tile, w_pair, preferred_element_type=jnp.f...]
    dynamic_slice x64 -> x0, local copies, waits for them, and re-layouts: 41.9 us -> none  [take(): lax.dynamic_index_in_dim(a, source, 0, False)]
    psum x1 -> x0, blocking collectives: 33.1 us -> none  [body(): lax.psum(own_counts.astype(jnp.bfloat16), 'col').astype(jnp.float32)]
    ppermute x4 -> x0, starting transfers between devices: 15.2 us -> none  [the longest x2 7.81 us: with_halo(): lax.ppermute(lax.slice_in_dim(block, block.shape[dim] - width, None, axis...]
  transfers between devices with their start and end apart: 11 -> 0, of which waited for: 8 -> 0; matrix products, arithmetic and copies ran while one was open for 3% -> 0% of each run, Pallas kernels for 0% -> 0%
where the time goes in v1:
time: 114 us
  Pallas kernels  110 us (96%)
  local copies, waits for them, and re-layouts  3.47 us (3%)
    pallas_call x1, Pallas kernels, body(): pl.pallas_call(kernel, out_shape=jax.ShapeDtypeStruct((3, 128), F32), in_...  110 us
    unnamed x2, local copies, waits for them, and re-layouts  3.47 us

profile of v1, /device:TPU:1, one launch (start us, length us, event | category | flops | bytes accessed | tf_op | source)
XLA Modules:
  0.0 113.5 jit_solution(6320787160340179067)
XLA Ops:
  0.0 2.2 %copy.19.tin_h = bf16[2,2,768,96]{3,2,1,0:T(8,128)(2,1)} copy(bf16[2,2,768,96]{2,3,1,0:T(8,128)(2,1)} %param.30) | data formatting | bytes 1179648 | tf_op args[12]
  2.2 110.0 %diffusion_step.1 = f32[3,128]{1,0:T(4,128)} custom-call(s32[4]{0:T(128)} %ws.1, s32[1,128]{1,0:T(1,128)} %bitcast.11, s32[12,128]{1,0:T(8,128)} %bitcast.9, bf16[128,128]{1,0:T(8,128)(2,1)} %x_in.1, bf16[32,128]{1,0:T(8,128)(2,1)} %bitcast.10, bf16[192,768]{1,0:T(8,128)(2,1)} %cond_h.1, bf16[192,96,128]{2,1,0:T(8,128)(2,1)} %pair_h.1, ...), custom_call_target="tpu_custom_call" | custom-call | tf_op jit(solution)/shard_map/diffusion_step/pallas_call | solution.py:680
  112.3 1.3 %copy.21 = f32[3,128]{1,0:T(4,128)} copy(f32[3,128]{1,0:T(4,128)} %diffusion_step.1) | data formatting | bytes 3072

commit v2 on v1

--- a/solution.py
+++ b/solution.py
@@ -16,6 +16,7 @@
 NCH = 8
 OWN = 6
 QT = 96
+BT = 8
 
 
 def dot(a, b):
@@ -103,7 +104,8 @@
     rsb,
     db,
     act,
-    acc,
+    feats,
+    hots,
     proj,
     lsem,
     h_ss,
@@ -167,18 +169,21 @@
     base = pl.multiple_of(base, 128)
     shift = QT * i - base
     ld_slab = [load(tok_in_h.at[:, :, pl.ds(base, 256)], slab)]
+    core_rows = pl.ds(pl.multiple_of(QT * k, 32), QT)
+    tin_k = tin.at[:, :, core_rows, :]
+    tout_k = tout.at[:, core_rows, :]
     ld_tok = [
-        load(tok_out_h, topad.at[:, 0:QT]),
-        load(tin_h, tin.at[k]),
-        load(tout_h, tout.at[k]),
+        load(tok_out_h.at[:, 32:96], topad.at[:, 0:64]),
+        load(tok_out_h.at[:, 0:32], topad.at[:, 96:128]),
+        load(tin_h, tin_k),
+        load(tout_h, tout_k),
         load(tok_atom_h, tok_atom),
         load(dec_in_h, dec_in),
         load(dec_out_h, dec_out),
         load(pos_h, pos),
     ]
 
-    topad[:, QT:, :] = jnp.zeros((16, 32, 768), BF16)
-    kv[:, :, :, QT:, :] = jnp.zeros((2, 16, 2, 32, 128), BF16)
+    topad[:, 64:96, :] = jnp.zeros((16, 32, 768), BF16)
     proj[...] = jnp.zeros((384, 128), BF16)
 
     bar = pltpu.get_barrier_semaphore()
@@ -213,8 +218,8 @@
     for cp in halo:
         cp.start()
     swap = [
-        rcopy(tin_h, tin.at[k], t_ss.at[0], t_rs.at[0], sib),
-        rcopy(tout_h, tout.at[k], t_ss.at[1], t_rs.at[1], sib),
+        rcopy(tin_h, tin_k, t_ss.at[0], t_rs.at[0], sib),
+        rcopy(tout_h, tout_k, t_ss.at[1], t_rs.at[1], sib),
     ]
     for cp in swap:
         cp.start()
@@ -223,29 +228,32 @@
         w = wt[...]
         for kb in range(3):
 
-            @pl.loop(0, 12)
+            @pl.loop(0, 24 // BT)
             def _(u):
-                t = 24 * kb + 2 * u
+                t = 24 * kb + BT * u
                 rows = []
-                for d in range(2):
+                for d in range(BT):
                     rows.append(pair[QT * kp + t + d])
-                    rows.append(pair[QT * kp + 72 + 2 * u + d, 32 * kb : 32 * kb + 32, :])
+                    rows.append(pair[QT * kp + 72 + BT * u + d, 32 * kb : 32 * kb + 32, :])
                 res = dot_t(w, jnp.concatenate(rows, 0))
                 zf = zb.reshape(32 * 144, 128)
-                for d in range(2):
+                for d in range(BT):
                     for g in range(4):
                         zf[pl.ds(g * 8 * 144 + kp * 72 + t + d, 8, stride=144), :] = res[
                             8 * g : 8 * g + 8, 128 * d : 128 * d + 128
                         ]
 
-    def bias_src(b, dev):
-        return zb.at[
-            pl.ds(16 * b + 2 * (dev // 2), 2), pl.ds(pl.multiple_of(72 * (dev % 2), 8), 72), :
-        ]
-
-    def bias_send(b, j):
-        dev = (c + j) % NC
-        return rcopy(bias_src(b, dev), bb.at[b, c], b_ss.at[b, j], b_rs.at[b, c], (r, dev))
+    def bias_src(b, ch, core):
+        return zb.at[pl.ds(16 * b + 2 * ch, 2), pl.ds(pl.multiple_of(72 * core, 8), 72), :]
+
+    def bias_send(b, j, core):
+        ch = (i + j) % NCH
+        return rcopy(
+            bias_src(b, ch, core), bb.at[b, c], b_ss.at[b, 2 * j + core], b_rs.at[b, c], (r, 2 * ch + core)
+        )
+
+    def bias_sib(b):
+        return rcopy(bias_src(b, i, 1 - k), bb.at[b, c], b_ss.at[b, 0], b_rs.at[b, c], sib)
 
     ld_pair[0].wait()
     ld_pair[1].wait()
@@ -300,52 +308,80 @@
     for cp in edge:
         cp.start()
 
+    b_send = [[], []]
+    for j in range(1, NCH):
+        b_send[0].append(bias_send(0, j, 0))
+        b_send[0][-1].start()
     ld_pair[2].wait()
     ld_pair[3].wait()
     bias_half(1)
-    b_send = [[bias_send(b, j) for j in range(1, NC)] for b in range(2)]
+    for j in range(1, NCH):
+        b_send[0].append(bias_send(0, j, 1))
+        b_send[0][-1].start()
+    b_send[0].append(bias_sib(0))
+    b_send[0][-1].start()
+    for j in range(1, NCH):
+        for core in range(2):
+            b_send[1].append(bias_send(1, j, core))
+    b_send[1].append(bias_sib(1))
     b_own = []
     for b in range(2):
-        cp = pltpu.make_async_copy(bias_src(b, c), bb.at[b, c], lsem.at[nload[0] + b])
+        cp = pltpu.make_async_copy(bias_src(b, i, k), bb.at[b, c], lsem.at[nload[0] + b])
         cp.start()
         b_own.append(cp)
-    for cp in b_send[0]:
-        cp.start()
+    bulk = list(b_send[1])
+
+    def some_bulk(n):
+        for _ in range(n):
+            if bulk:
+                bulk.pop(0).start()
 
     for cp in ld_slab:
         cp.wait()
-    pick = jnp.logical_and(
-        iota((256, 128), 0) == iota((256, 128), 1) + shift, iota((256, 128), 1) < QT
-    )
-    pick = jnp.where(pick, 1.0, 0.0).astype(BF16)
-
-    @pl.loop(0, 8)
+    e_row = iota((256, 256), 0) - shift
+    e_col = iota((256, 256), 1)
+
+    def picker(lo, hi, first):
+        hit = jnp.logical_and(e_col >= lo, e_col < hi)
+        return jnp.logical_and(hit, e_row == e_col - lo + first)
+
+    def onehot(m):
+        return jnp.where(m, 1.0, 0.0).astype(BF16)
+
+    pick_q = onehot(picker(0, 96, 0))
+    pick_g = onehot(jnp.logical_or(picker(128, 192, 32), picker(224, 256, 0)))
+    pick_k = onehot(picker(0, 96, 0))
+    pick_v = onehot(picker(96, 192, 0))
+
+    @pl.loop(0, 2)
     def _(m):
-        wq[m] = dot(slab[m], pick).astype(BF16)
-
+        wq[2 * m] = (dot(slab[4 * m], pick_q) + dot(slab[4 * m + 3], pick_g)).astype(BF16)
+        wq[2 * m + 1] = (dot(slab[4 * m + 1], pick_k) + dot(slab[4 * m + 2], pick_v)).astype(BF16)
+
+    for cp in ld_pool:
+        cp.wait()
+    want = (iota((QT, 128), 0) + QT * k).astype(F32)
+
+    def pool_slot(s):
+        feats[s] = jnp.maximum(dot(x1all[s, 16:144, :], pool[...]), 0.0).astype(BF16)
+        t = x1all[s, 0:16, :].astype(F32)[0:1]
+        hots[s] = jnp.where(t == want, 1.0, 0.0).astype(BF16)
+
+    pool_slot(c)
     for j in range(1, NCH):
         s = 2 * ((i + j) % NCH) + k
         rcopy(x1_slot(s), x1_slot(s), x_ss.at[0], x_rs.at[s], sib).wait_recv()
         x_fwd[j].start()
-    for cp in x_far:
-        cp.wait_recv()
-    for cp in ld_pool:
-        cp.wait()
-    acc[...] = jnp.zeros((QT, 768), F32)
-
-    def pool_step(s2, cnt):
-        both = jnp.concatenate([x1all[2 * s2, 16:144, :], x1all[2 * s2 + 1, 16:144, :]], 0)
-        feats = jnp.maximum(dot(both, pool[...]), 0.0).astype(BF16)
-        hots = []
-        want = (iota((QT, 128), 0) + QT * k).astype(F32)
-        for d in range(2):
-            t = x1all[2 * s2 + d, 0:16, :].astype(F32)[0:1]
-            hots.append(jnp.where(t == want, 1.0, 0.0))
-        acc[...] += dot(jnp.concatenate(hots, 1).astype(BF16), feats)
-        return cnt + hots[0] + hots[1]
-
-    cnt = lax.fori_loop(0, 8, pool_step, jnp.zeros((QT, 128), F32))
-    act[...] = acc[...] / jnp.sum(cnt, -1, keepdims=True) + cond[...].astype(F32)
+        pool_slot(s)
+    for j in range(NCH):
+        x_far[j].wait_recv()
+        pool_slot(2 * ((i + j) % NCH) + 1 - k)
+    hot_all = jnp.concatenate([hots[s] for s in range(NC)], 1)
+    cnt = hots[0].astype(F32)
+    for s in range(1, NC):
+        cnt = cnt + hots[s].astype(F32)
+    sums = dot(hot_all, feats[...].reshape(NC * 128, 768))
+    act[...] = sums / jnp.sum(cnt, -1, keepdims=True) + cond[...].astype(F32)
 
     nvalid = jnp.sum(
         jnp.sum(mask[...].astype(F32), 1, keepdims=True), 0, keepdims=True
@@ -354,14 +390,23 @@
     lanef = lane.astype(F32)
     mine = 2 * r + k
 
+    left = jnp.where(lane < 64, 1.0, 0.0).astype(BF16)
+    right = jnp.where(lane < 64, 0.0, 1.0).astype(BF16)
+    pad = jnp.zeros((32, 128), BF16)
+    lq = iota((QT, 128), 1)
+
     def kv_slot(b, s):
-        return kv.at[b, s, :, 0:QT, :]
+        return kv.at[b, s]
 
     pend = []
     for b in range(2):
         n = normed(act[...]).astype(BF16)
-        kv[b, mine, 0, 0:QT, :] = dot(n, wq[4 * b + 1]).astype(BF16)
-        kv[b, mine, 1, 0:QT, :] = dot(n, wq[4 * b + 2]).astype(BF16)
+        own_kv = dot(n, wq[2 * b + 1])
+        kv[b, mine, 0] = own_kv[0:48, 0:128].astype(BF16)
+        kv[b, mine, 1] = jnp.where(
+            lane < 64, own_kv[0:48, 128:256], pltpu.roll(own_kv[48:96, 128:256], 64, 1)
+        ).astype(BF16)
+        kv[b, mine, 2] = own_kv[48:96, 0:128].astype(BF16)
         for j in range(1, NR):
             cp = rcopy(
                 kv_slot(b, mine),
@@ -380,36 +425,23 @@
             )
         fwd[0].start()
         pend += fwd
-        q = dot(n, wq[4 * b]).astype(BF16).astype(F32)
-        gate = dot(n, wq[4 * b + 3])
-        lq = iota((QT, 128), 1)
-        qs = jnp.concatenate(
-            [
-                jnp.where(lq < 48, q, 0.0),
-                jnp.where(lq < 48, 0.0, q),
-            ],
-            0,
-        ).astype(BF16)
+        qg = dot(n, wq[2 * b])
+        q = qg[:, 0:128].astype(BF16).astype(F32)
+        gate = jax.nn.sigmoid(qg[:, 128:256])
+        qs = jnp.concatenate([jnp.where(lq < 48, q, 0.0), jnp.where(lq < 48, 0.0, q)], 0).astype(
+            BF16
+        )
         b_own[b].wait()
         for j in range(1, NC):
             s = (c + j) % NC
             rcopy(bb.at[b, s], bb.at[b, s], b_ss.at[b, 0], b_rs.at[b, s], sib).wait_recv()
-        for j in range(1, NR):
-            s = 2 * ((r + j) % NR) + k
-            rcopy(kv_slot(b, s), kv_slot(b, s), kv_ss.at[b, 0], kv_rs.at[b, s], sib).wait_recv()
-            fwd[j].start()
-        for j in range(NR):
-            s = 2 * ((r + j) % NR) + 1 - k
-            rcopy(kv_slot(b, s), kv_slot(b, s), kv_ss.at[b, 0], kv_rs.at[b, s], sib).wait_recv()
-        if b == 0:
-            for cp in b_send[1]:
-                cp.start()
-
-        def score_step(s2, mx):
-            keys = jnp.concatenate([kv[b, 2 * s2, 0], kv[b, 2 * s2 + 1, 0]], 0)
-            s = dot_t(qs, keys) * (1.0 / math.sqrt(48.0))
-            for d in range(2):
-                slot = 2 * s2 + d
+
+        def scores(slots, mx):
+            keys = []
+            for s in slots:
+                keys += [kv[b, s, 0], kv[b, s, 2], pad]
+            dots = dot_t(qs, jnp.concatenate(keys, 0)) * (1.0 / math.sqrt(48.0))
+            for d, slot in enumerate(slots):
                 first = (QT * slot).astype(F32)
                 ok = lanef + first < jnp.minimum(nvalid, first + QT)
                 parts = []
@@ -423,32 +455,61 @@
                         ),
                     )
                     parts += [m, tail]
-                sc = jnp.where(ok, s[:, 128 * d : 128 * d + 128] + jnp.concatenate(parts, 0), NEG)
+                sc = dots[:, 128 * d : 128 * d + 128] + jnp.concatenate(parts, 0)
+                sc = jnp.where(ok, sc, NEG)
                 ssc[slot] = sc
                 mx = jnp.maximum(mx, sc)
             return mx
 
-        mx = lax.fori_loop(0, 8, score_step, jnp.full((2 * QT, 128), 2 * NEG, F32))
+        mx = jnp.full((2 * QT, 128), 2 * NEG, F32)
+        for grp in range(4):
+            slots = []
+            for j in (2 * grp, 2 * grp + 1):
+                s = 2 * ((r + j) % NR) + k
+                slots.append(s)
+                if j > 0:
+                    rcopy(
+                        kv_slot(b, s), kv_slot(b, s), kv_ss.at[b, 0], kv_rs.at[b, s], sib
+                    ).wait_recv()
+                    fwd[j].start()
+            for j in (2 * grp, 2 * grp + 1):
+                s = 2 * ((r + j) % NR) + 1 - k
+                slots.append(s)
+                rcopy(kv_slot(b, s), kv_slot(b, s), kv_ss.at[b, 0], kv_rs.at[b, s], sib).wait_recv()
+            mx = scores(slots, mx)
+        if b == 0:
+            some_bulk(3)
         top = jnp.max(mx, -1, keepdims=True)
 
-        def value_step(s2, state):
+        def value_step(s4, state):
             tot, o = state
-            e0 = jnp.exp(ssc[2 * s2] - top)
-            e1 = jnp.exp(ssc[2 * s2 + 1] - top)
-            p = jnp.concatenate([e0, e1], 1).astype(BF16)
-            vals = jnp.concatenate([kv[b, 2 * s2, 1], kv[b, 2 * s2 + 1, 1]], 0)
-            return tot + (e0 + e1), o + dot(p, vals)
-
-        zero = jnp.zeros((2 * QT, 128), F32)
-        tot, o = lax.fori_loop(0, 8, value_step, (zero, zero))
-        o = o / jnp.sum(tot, -1, keepdims=True)
-        o = jnp.where(lq < 48, o[:QT], o[QT:])
-        ob[b, i] = (jax.nn.sigmoid(gate) * o).astype(BF16)
+            ps = []
+            vals = []
+            for d in range(4):
+                s = 4 * s4 + d
+                e = jnp.exp(ssc[s] - top)
+                tot = tot + e
+                ps.append(e.astype(BF16))
+                mid = kv[b, s, 1]
+                vals.append(jnp.concatenate([kv[b, s, 0], mid * left], 1))
+                vals.append(jnp.concatenate([kv[b, s, 2], mid * right], 1))
+                vals.append(jnp.concatenate([pad, pad], 1))
+            return tot, o + dot(jnp.concatenate(ps, 1), jnp.concatenate(vals, 0))
+
+        tot, o = lax.fori_loop(
+            0, 4, value_step, (jnp.zeros((2 * QT, 128), F32), jnp.zeros((2 * QT, 256), F32))
+        )
+        inv = 1.0 / jnp.sum(tot, -1, keepdims=True)
+        o_a = o[:QT, 0:128] * inv[:QT]
+        o_b = (o[:, 128:256] + pltpu.roll(o[:, 128:256], 64, 1)) * inv
+        o = jnp.where(lq < 16, o_b[:QT], jnp.where(lq < 64, o_b[QT:], jnp.where(lq < 96, 0.0, o_a)))
+        ob[b, i] = (gate * o).astype(BF16)
         for j in range(1, NCH):
             cp = rcopy(ob.at[b, i], ob.at[b, i], o_ss.at[b, j], o_rs.at[b, i], chip(j))
             cp.start()
             pend.append(cp)
         if b == 0:
+            some_bulk(4)
             for cp in ld_tok:
                 cp.wait()
             for cp in swap:
@@ -460,12 +521,9 @@
         act[...] += dot(gated, topad[8 * b : 8 * b + 8].reshape(1024, 768))
 
         m = normed(act[...]).astype(BF16)
-        part = jnp.zeros((QT, 768), F32)
-        for s in range(2):
-            swish = jax.nn.silu(dot(m, tin[s, b, 0]))
-            hidden = (swish * dot(m, tin[s, b, 1])).astype(BF16)
-            part = part + dot(hidden, tout[s, b])
-        prt[b] = part.astype(BF16)
+        swish = jax.nn.silu(dot_t(m, tin[b, 0]))
+        hidden = (swish * dot_t(m, tin[b, 1])).astype(BF16)
+        prt[b] = dot(hidden, tout[b]).astype(BF16)
         for o_ in range(OWN):
 
             @pl.when(i != o_)
@@ -477,6 +535,9 @@
                     r_rs.at[b, i],
                     (r, 2 * o_ + k),
                 ).start()
+
+        if b == 0:
+            some_bulk(4)
 
         @pl.when(is_owner)
         def _():
@@ -525,6 +586,7 @@
                     ).start()
 
         if b == 0:
+            some_bulk(4)
             for o_ in range(OWN):
 
                 @pl.when(i != o_)
@@ -633,10 +695,10 @@
         V((128, 128), BF16),
         V((128, 768), BF16),
         V((8, 768, 256), BF16),
-        V((8, 768, 128), BF16),
+        V((4, 768, 256), BF16),
         V((16, 128, 768), BF16),
-        V((2, 2, 2, 768, 96), BF16),
-        V((2, 2, 96, 768), BF16),
+        V((2, 2, 192, 768), BF16),
+        V((2, 192, 768), BF16),
         V((768, 128), BF16),
         V((4, 128, 128), BF16),
         V((128, 128), BF16),
@@ -646,14 +708,15 @@
         V((2, 80, 128), BF16),
         V((32, 144, 128), F32),
         V((2, 16, 2, 72, 128), F32),
-        V((2, 16, 2, 128, 128), BF16),
+        V((2, 16, 3, 48, 128), BF16),
         V((16, 192, 128), F32),
         V((2, 8, QT, 128), BF16),
         V((2, QT, 768), BF16),
         V((2, 8, 16, 768), BF16),
         V((6, 16, 768), BF16),
         V((QT, 768), F32),
-        V((QT, 768), F32),
+        V((16, 128, 768), BF16),
+        V((16, QT, 128), BF16),
         V((384, 128), BF16),
         dma((24,)),
         dma((2,)),
@@ -700,7 +763,7 @@
         pool_weight,
         tok_in.reshape(8, 768, 768),
         tok_out.reshape(16, 96, 768),
-        trans_in,
+        jnp.swapaxes(trans_in, 2, 3),
         trans_out,
         tok_atom,
         dec_in,

time: 114 us -> 101 us (0.89)
  Pallas kernels: 110 us -> 99.8 us
  local copies, waits for them, and re-layouts: 3.47 us -> 1.26 us
    pallas_call x1, Pallas kernels: 110 us -> 99.8 us  [body(): pl.pallas_call(kernel, out_shape=jax.ShapeDtypeStruct((3, 128), F32), in_...]
    unnamed x2 -> x1, local copies, waits for them, and re-layouts: 3.47 us -> 1.26 us
where the time goes in v2:
time: 101 us
  Pallas kernels  99.8 us (99%)
  local copies, waits for them, and re-layouts  1.26 us (1%)
    pallas_call x1, Pallas kernels, body(): pl.pallas_call(kernel, out_shape=jax.ShapeDtypeStruct((3, 128), F32), in_...  99.8 us

profile of v2, /device:TPU:1, one launch (start us, length us, event | category | flops | bytes accessed | tf_op | source)
XLA Modules:
  0.0 101.1 jit_solution(15098829510041095315)
XLA Ops:
  0.0 99.8 %diffusion_step.1 = f32[3,128]{1,0:T(4,128)} custom-call(s32[4]{0:T(128)} %ws.1, s32[1,128]{1,0:T(1,128)} %bitcast.13, s32[12,128]{1,0:T(8,128)} %bitcast.11, bf16[128,128]{1,0:T(8,128)(2,1)} %x_in.1, bf16[32,128]{1,0:T(8,128)(2,1)} %bitcast.12, bf16[192,768]{1,0:T(8,128)(2,1)} %cond_h.1, bf16[192,96,128]{2,1,0:T(8,128)(2,1)} %pair_h.1, ...), custom_call_target="tpu_custom_call" | custom-call | tf_op jit(solution)/shard_map/diffusion_step/pallas_call | solution.py:743
  99.8 1.3 %copy.20 = f32[3,128]{1,0:T(4,128)} copy(f32[3,128]{1,0:T(4,128)} %diffusion_step.1) | data formatting | bytes 3072

commit v3 on v2

--- a/solution.py
+++ b/solution.py
@@ -16,6 +16,8 @@
 NCH = 8
 OWN = 6
 QT = 96
+G0, G1, G2 = 5, 4, 4
+EARLY = 6
 BT = 8
 
 
@@ -186,44 +188,6 @@
     topad[:, 64:96, :] = jnp.zeros((16, 32, 768), BF16)
     proj[...] = jnp.zeros((384, 128), BF16)
 
-    bar = pltpu.get_barrier_semaphore()
-
-    def greet(dev):
-        pl.semaphore_signal(bar, inc=1, device_id=dev, device_id_type=MESH)
-
-    for j in range(1, NC):
-        greet((r, (c + j) % NC))
-    for j in range(1, NR):
-        greet(((r + j) % NR, c))
-    greet(nxt)
-    greet(prv)
-
-    @pl.when(c == 0)
-    def _():
-        for o in (5, 7, 9, 11):
-            greet(((r + NR - 1) % NR, o))
-
-    @pl.when(c == NC - 1)
-    def _():
-        for o in (0, 2, 4, 6):
-            greet(((r + 1) % NR, o))
-
-    extra = jnp.where(jnp.logical_or(is_tail, is_head), 1, 0)
-    pl.semaphore_wait(bar, 24 + extra)
-
-    halo = [
-        rcopy(x_in.at[64:128], xh.at[1], h_ss.at[0], h_rs.at[1], nxt),
-        rcopy(x_in.at[0:64], xh.at[0], h_ss.at[1], h_rs.at[0], prv),
-    ]
-    for cp in halo:
-        cp.start()
-    swap = [
-        rcopy(tin_h, tin_k, t_ss.at[0], t_rs.at[0], sib),
-        rcopy(tout_h, tout_k, t_ss.at[1], t_rs.at[1], sib),
-    ]
-    for cp in swap:
-        cp.start()
-
     def bias_half(kp):
         w = wt[...]
         for kb in range(3):
@@ -243,6 +207,47 @@
                             8 * g : 8 * g + 8, 128 * d : 128 * d + 128
                         ]
 
+    bar = pltpu.get_barrier_semaphore()
+
+    def greet(dev):
+        pl.semaphore_signal(bar, inc=1, device_id=dev, device_id_type=MESH)
+
+    for j in range(1, NC):
+        greet((r, (c + j) % NC))
+    for j in range(1, NR):
+        greet(((r + j) % NR, c))
+    greet(nxt)
+    greet(prv)
+
+    @pl.when(c == 0)
+    def _():
+        for o in (5, 7, 9, 11):
+            greet(((r + NR - 1) % NR, o))
+
+    @pl.when(c == NC - 1)
+    def _():
+        for o in (0, 2, 4, 6):
+            greet(((r + 1) % NR, o))
+
+    ld_pair[0].wait()
+    ld_pair[1].wait()
+    bias_half(0)
+    extra = jnp.where(jnp.logical_or(is_tail, is_head), 1, 0)
+    pl.semaphore_wait(bar, 24 + extra)
+
+    halo = [
+        rcopy(x_in.at[64:128], xh.at[1], h_ss.at[0], h_rs.at[1], nxt),
+        rcopy(x_in.at[0:64], xh.at[0], h_ss.at[1], h_rs.at[0], prv),
+    ]
+    for cp in halo:
+        cp.start()
+    swap = [
+        rcopy(tin_h, tin_k, t_ss.at[0], t_rs.at[0], sib),
+        rcopy(tout_h, tout_k, t_ss.at[1], t_rs.at[1], sib),
+    ]
+    for cp in swap:
+        cp.start()
+
     def bias_src(b, ch, core):
         return zb.at[pl.ds(16 * b + 2 * ch, 2), pl.ds(pl.multiple_of(72 * core, 8), 72), :]
 
@@ -255,9 +260,28 @@
     def bias_sib(b):
         return rcopy(bias_src(b, i, 1 - k), bb.at[b, c], b_ss.at[b, 0], b_rs.at[b, c], sib)
 
-    ld_pair[0].wait()
-    ld_pair[1].wait()
-    bias_half(0)
+    ring = (2, 6, 4, 1, 7, 3, 5)
+    b_send = [[], []]
+    for b in range(2):
+        for core in range(2):
+            b_send[b] += [bias_send(b, j, core) for j in ring]
+        b_send[b].append(bias_sib(b))
+    bulk = b_send[0] + b_send[1]
+
+    def some_bulk(n):
+        for _ in range(n):
+            if bulk:
+                bulk.pop(0).start()
+
+    some_bulk(EARLY)
+    ld_pair[2].wait()
+    ld_pair[3].wait()
+    bias_half(1)
+    b_own = []
+    for b in range(2):
+        cp = pltpu.make_async_copy(bias_src(b, i, k), bb.at[b, c], lsem.at[nload[0] + b])
+        cp.start()
+        b_own.append(cp)
 
     for cp in ld_enc:
         cp.wait()
@@ -308,34 +332,6 @@
     for cp in edge:
         cp.start()
 
-    b_send = [[], []]
-    for j in range(1, NCH):
-        b_send[0].append(bias_send(0, j, 0))
-        b_send[0][-1].start()
-    ld_pair[2].wait()
-    ld_pair[3].wait()
-    bias_half(1)
-    for j in range(1, NCH):
-        b_send[0].append(bias_send(0, j, 1))
-        b_send[0][-1].start()
-    b_send[0].append(bias_sib(0))
-    b_send[0][-1].start()
-    for j in range(1, NCH):
-        for core in range(2):
-            b_send[1].append(bias_send(1, j, core))
-    b_send[1].append(bias_sib(1))
-    b_own = []
-    for b in range(2):
-        cp = pltpu.make_async_copy(bias_src(b, i, k), bb.at[b, c], lsem.at[nload[0] + b])
-        cp.start()
-        b_own.append(cp)
-    bulk = list(b_send[1])
-
-    def some_bulk(n):
-        for _ in range(n):
-            if bulk:
-                bulk.pop(0).start()
-
     for cp in ld_slab:
         cp.wait()
     e_row = iota((256, 256), 0) - shift
@@ -358,30 +354,43 @@
         wq[2 * m] = (dot(slab[4 * m], pick_q) + dot(slab[4 * m + 3], pick_g)).astype(BF16)
         wq[2 * m + 1] = (dot(slab[4 * m + 1], pick_k) + dot(slab[4 * m + 2], pick_v)).astype(BF16)
 
+    some_bulk(15 - EARLY)
     for cp in ld_pool:
         cp.wait()
     want = (iota((QT, 128), 0) + QT * k).astype(F32)
 
-    def pool_slot(s):
-        feats[s] = jnp.maximum(dot(x1all[s, 16:144, :], pool[...]), 0.0).astype(BF16)
+    def pool_slot(s, n):
+        feats[n] = jnp.maximum(dot(x1all[s, 16:144, :], pool[...]), 0.0).astype(BF16)
         t = x1all[s, 0:16, :].astype(F32)[0:1]
-        hots[s] = jnp.where(t == want, 1.0, 0.0).astype(BF16)
-
-    pool_slot(c)
-    for j in range(1, NCH):
+        hots[n] = jnp.where(t == want, 1.0, 0.0).astype(BF16)
+
+    def pool_group(g):
+        hot = jnp.concatenate([hots[4 * g + d] for d in range(4)], 1)
+        part = dot(hot, feats[4 * g : 4 * g + 4].reshape(512, 768))
+        n = hot[:, 0:128].astype(F32)
+        for d in range(1, 4):
+            n = n + hot[:, 128 * d : 128 * d + 128].astype(F32)
+        if g == 0:
+            act[...] = part
+        else:
+            act[...] += part
+        return n
+
+    cnt = jnp.zeros((QT, 128), F32)
+    for j in range(NCH):
         s = 2 * ((i + j) % NCH) + k
-        rcopy(x1_slot(s), x1_slot(s), x_ss.at[0], x_rs.at[s], sib).wait_recv()
-        x_fwd[j].start()
-        pool_slot(s)
+        if j > 0:
+            rcopy(x1_slot(s), x1_slot(s), x_ss.at[0], x_rs.at[s], sib).wait_recv()
+            x_fwd[j].start()
+        pool_slot(s, j)
+        if j % 4 == 3:
+            cnt = cnt + pool_group(j // 4)
     for j in range(NCH):
         x_far[j].wait_recv()
-        pool_slot(2 * ((i + j) % NCH) + 1 - k)
-    hot_all = jnp.concatenate([hots[s] for s in range(NC)], 1)
-    cnt = hots[0].astype(F32)
-    for s in range(1, NC):
-        cnt = cnt + hots[s].astype(F32)
-    sums = dot(hot_all, feats[...].reshape(NC * 128, 768))
-    act[...] = sums / jnp.sum(cnt, -1, keepdims=True) + cond[...].astype(F32)
+        pool_slot(2 * ((i + j) % NCH) + 1 - k, NCH + j)
+        if j % 4 == 3:
+            cnt = cnt + pool_group(2 + j // 4)
+    act[...] = act[...] / jnp.sum(cnt, -1, keepdims=True) + cond[...].astype(F32)
 
     nvalid = jnp.sum(
         jnp.sum(mask[...].astype(F32), 1, keepdims=True), 0, keepdims=True
@@ -431,6 +440,10 @@
         qs = jnp.concatenate([jnp.where(lq < 48, q, 0.0), jnp.where(lq < 48, 0.0, q)], 0).astype(
             BF16
         )
+        for j in range(1, NR):
+            s = 2 * ((r + j) % NR) + k
+            rcopy(kv_slot(b, s), kv_slot(b, s), kv_ss.at[b, 0], kv_rs.at[b, s], sib).wait_recv()
+            fwd[j].start()
         b_own[b].wait()
         for j in range(1, NC):
             s = (c + j) % NC
@@ -462,23 +475,18 @@
             return mx
 
         mx = jnp.full((2 * QT, 128), 2 * NEG, F32)
+        if b == 0:
+            some_bulk(G0)
         for grp in range(4):
             slots = []
             for j in (2 * grp, 2 * grp + 1):
                 s = 2 * ((r + j) % NR) + k
                 slots.append(s)
-                if j > 0:
-                    rcopy(
-                        kv_slot(b, s), kv_slot(b, s), kv_ss.at[b, 0], kv_rs.at[b, s], sib
-                    ).wait_recv()
-                    fwd[j].start()
             for j in (2 * grp, 2 * grp + 1):
                 s = 2 * ((r + j) % NR) + 1 - k
                 slots.append(s)
                 rcopy(kv_slot(b, s), kv_slot(b, s), kv_ss.at[b, 0], kv_rs.at[b, s], sib).wait_recv()
             mx = scores(slots, mx)
-        if b == 0:
-            some_bulk(3)
         top = jnp.max(mx, -1, keepdims=True)
 
         def value_step(s4, state):
@@ -509,7 +517,7 @@
             cp.start()
             pend.append(cp)
         if b == 0:
-            some_bulk(4)
+            some_bulk(G1)
             for cp in ld_tok:
                 cp.wait()
             for cp in swap:
@@ -537,7 +545,7 @@
                 ).start()
 
         if b == 0:
-            some_bulk(4)
+            some_bulk(G2)
 
         @pl.when(is_owner)
         def _():
@@ -586,7 +594,7 @@
                     ).start()
 
         if b == 0:
-            some_bulk(4)
+            some_bulk(15)
             for o_ in range(OWN):
 
                 @pl.when(i != o_)

time: 101 us -> 92 us (0.911)
  Pallas kernels: 99.8 us -> 90.6 us
    pallas_call x1, Pallas kernels: 99.8 us -> 90.6 us  [body(): pl.pallas_call(kernel, out_shape=jax.ShapeDtypeStruct((3, 128), F32), in_...]
where the time goes in v3:
time: 92 us; the launch traced here: 91.9 us
  Pallas kernels  90.6 us (98%)
  local copies, waits for them, and re-layouts  1.26 us (1%)
    pallas_call x1, Pallas kernels, body(): pl.pallas_call(kernel, out_shape=jax.ShapeDtypeStruct((3, 128), F32), in_...  90.6 us

profile of v3, /device:TPU:1, one launch (start us, length us, event | category | flops | bytes accessed | tf_op | source)
XLA Modules:
  0.0 91.9 jit_solution(10305933089829567149)
XLA Ops:
  0.0 90.6 %diffusion_step.1 = f32[3,128]{1,0:T(4,128)} custom-call(s32[4]{0:T(128)} %ws.1, s32[1,128]{1,0:T(1,128)} %bitcast.13, s32[12,128]{1,0:T(8,128)} %bitcast.11, bf16[128,128]{1,0:T(8,128)(2,1)} %x_in.1, bf16[32,128]{1,0:T(8,128)(2,1)} %bitcast.12, bf16[192,768]{1,0:T(8,128)(2,1)} %cond_h.1, bf16[192,96,128]{2,1,0:T(8,128)(2,1)} %pair_h.1, ...), custom_call_target="tpu_custom_call" | custom-call | tf_op jit(solution)/shard_map/diffusion_step/pallas_call | solution.py:751
  90.6 1.3 %copy.20 = f32[3,128]{1,0:T(4,128)} copy(f32[3,128]{1,0:T(4,128)} %diffusion_step.1) | data formatting | bytes 3072

commit v4 on v3

--- a/solution.py
+++ b/solution.py
@@ -14,10 +14,22 @@
 NR = 8
 NC = 16
 NCH = 8
+FAR_FIRST = (5, 3, 4, 1, 7, 2, 6)
 OWN = 6
+CHIP_OF = (0, 3, 6, 5, 2, 1)
 QT = 96
-G0, G1, G2 = 5, 4, 4
-EARLY = 6
+BULK = (
+    ((0, 2, 0), (0, 6, 0), (0, 4, 0), (0, 1, 0), (0, 7, 0), (0, 3, 0)),
+    (),
+    ((0, 5, 0), (0, 2, 1), (0, 6, 1), (0, 4, 1), (0, 1, 1), (0, 7, 1), (0, 3, 1), (0, 5, 1), (0, 0, 0)),
+    ((1, 2, 0), (1, 6, 0), (1, 4, 0)),
+    ((1, 1, 0), (1, 1, 1), (1, 4, 1)),
+    ((1, 7, 0), (1, 7, 1)),
+    ((1, 3, 0), (1, 3, 1)),
+    ((1, 5, 0), (1, 5, 1)),
+    ((1, 2, 1), (1, 6, 1), (1, 0, 0)),
+)
+ZR = 80
 BT = 8
 
 
@@ -101,6 +113,7 @@
     bb,
     kv,
     ssc,
+    vb,
     ob,
     prt,
     rsb,
@@ -141,9 +154,17 @@
     prv = (flat + NR * NC - 1) % (NR * NC)
     nxt = (nxt // NC, nxt % NC)
     prv = (prv // NC, prv % NC)
-    is_owner = i < OWN
-    is_tail = jnp.logical_and(k == 1, jnp.logical_and(i >= 2, i < OWN))
-    is_head = jnp.logical_and(k == 0, i < 4)
+    turned = (i + 4 * k) % NCH
+    unit = OWN + 0 * i
+    for u in range(OWN):
+        unit = jnp.where(turned == CHIP_OF[u], u, unit)
+    is_owner = unit < OWN
+    is_tail = jnp.logical_and(k == 1, jnp.logical_and(unit >= 2, is_owner))
+    is_head = jnp.logical_and(k == 0, unit < 4)
+
+    def owner_dev(u):
+        return (r, 2 * ((CHIP_OF[u] + 4 * k) % NCH) + k)
+
 
     def chip(j):
         return (r, 2 * ((i + j) % NCH) + k)
@@ -185,27 +206,50 @@
         load(pos_h, pos),
     ]
 
+    zb[:, :, 72:, :] = jnp.zeros((16, 2, 8, 128), jnp.int32)
+    vb[:, 96:128, :] = jnp.zeros((16, 32, 256), BF16)
     topad[:, 64:96, :] = jnp.zeros((16, 32, 768), BF16)
     proj[...] = jnp.zeros((384, 128), BF16)
 
+    order = iota((32, 32), 1) == 16 * (iota((32, 32), 0) // 16) + 2 * (iota((32, 32), 0) % 8) + (
+        iota((32, 32), 0) // 8
+    ) % 2
+    w_heads = dot(jnp.where(order, 1.0, 0.0).astype(BF16), wt[...]).astype(BF16)
+    lane32 = iota((32, 128), 1)
+    zf = zb.reshape(16 * 2 * ZR, 128)
+
     def bias_half(kp):
-        w = wt[...]
+        def words(u, first):
+            return lax.shift_left(u[first : first + 8], 16) | u[first + 8 : first + 16]
+
+        def put(b, row, value):
+            zf[pl.ds(b * 16 * ZR + kp * ZR + row, 8, stride=2 * ZR), :] = value
+
+        sizes = jnp.zeros((32, 128), jnp.int32)
         for kb in range(3):
 
-            @pl.loop(0, 24 // BT)
-            def _(u):
-                t = 24 * kb + BT * u
+            def tiles(n, sizes):
+                t = 24 * kb + BT * n
                 rows = []
                 for d in range(BT):
                     rows.append(pair[QT * kp + t + d])
-                    rows.append(pair[QT * kp + 72 + BT * u + d, 32 * kb : 32 * kb + 32, :])
-                res = dot_t(w, jnp.concatenate(rows, 0))
-                zf = zb.reshape(32 * 144, 128)
+                    rows.append(pair[QT * kp + 72 + BT * n + d, 32 * kb : 32 * kb + 32, :])
+                res = dot_t(w_heads, jnp.concatenate(rows, 0))
                 for d in range(BT):
-                    for g in range(4):
-                        zf[pl.ds(g * 8 * 144 + kp * 72 + t + d, 8, stride=144), :] = res[
-                            8 * g : 8 * g + 8, 128 * d : 128 * d + 128
-                        ]
+                    x = res[:, 128 * d : 128 * d + 128]
+                    most = jnp.max(jnp.abs(x), -1, keepdims=True)
+                    size = (most * (65536.0 * 1.000001)).astype(jnp.int32) + 1
+                    sizes = sizes + jnp.where(lane32 == t + d, size, 0)
+                    inv = (32767.0 * 65536.0) / size.astype(F32)
+                    u = (x * inv + 32768.5).astype(jnp.int32)
+                    for b in range(2):
+                        put(b, t + d, words(u, 16 * b))
+                return sizes
+
+            sizes = lax.fori_loop(0, 24 // BT, tiles, sizes)
+        for b in range(2):
+            for odd in range(2):
+                put(b, 72 + odd, sizes[16 * b + 8 * odd : 16 * b + 8 * odd + 8])
 
     bar = pltpu.get_barrier_semaphore()
 
@@ -221,13 +265,13 @@
 
     @pl.when(c == 0)
     def _():
-        for o in (5, 7, 9, 11):
-            greet(((r + NR - 1) % NR, o))
+        for u in range(2, OWN):
+            greet(((r + NR - 1) % NR, 2 * ((CHIP_OF[u] + 4) % NCH) + 1))
 
     @pl.when(c == NC - 1)
     def _():
-        for o in (0, 2, 4, 6):
-            greet(((r + 1) % NR, o))
+        for u in range(4):
+            greet(((r + 1) % NR, 2 * CHIP_OF[u]))
 
     ld_pair[0].wait()
     ld_pair[1].wait()
@@ -249,7 +293,7 @@
         cp.start()
 
     def bias_src(b, ch, core):
-        return zb.at[pl.ds(16 * b + 2 * ch, 2), pl.ds(pl.multiple_of(72 * core, 8), 72), :]
+        return zb.at[8 * b + ch, core]
 
     def bias_send(b, j, core):
         ch = (i + j) % NCH
@@ -260,20 +304,14 @@
     def bias_sib(b):
         return rcopy(bias_src(b, i, 1 - k), bb.at[b, c], b_ss.at[b, 0], b_rs.at[b, c], sib)
 
-    ring = (2, 6, 4, 1, 7, 3, 5)
-    b_send = [[], []]
-    for b in range(2):
-        for core in range(2):
-            b_send[b] += [bias_send(b, j, core) for j in ring]
-        b_send[b].append(bias_sib(b))
-    bulk = b_send[0] + b_send[1]
-
-    def some_bulk(n):
-        for _ in range(n):
-            if bulk:
-                bulk.pop(0).start()
-
-    some_bulk(EARLY)
+    b_sent = []
+
+    def some_bulk(when):
+        for b, j, core in BULK[when]:
+            b_sent.append(bias_sib(b) if j == 0 else bias_send(b, j, core))
+            b_sent[-1].start()
+
+    some_bulk(0)
     ld_pair[2].wait()
     ld_pair[3].wait()
     bias_half(1)
@@ -283,6 +321,7 @@
         cp.start()
         b_own.append(cp)
 
+    some_bulk(1)
     for cp in ld_enc:
         cp.wait()
     for cp in halo:
@@ -316,7 +355,7 @@
         return x1all.at[s, 0:144]
 
     x_send = [
-        rcopy(x1_slot(c), x1_slot(c), x_ss.at[j], x_rs.at[c], chip(j)) for j in range(1, NCH)
+        rcopy(x1_slot(c), x1_slot(c), x_ss.at[j], x_rs.at[c], chip(j)) for j in FAR_FIRST
     ]
     x_fwd = []
     for j in range(NCH):
@@ -354,7 +393,7 @@
         wq[2 * m] = (dot(slab[4 * m], pick_q) + dot(slab[4 * m + 3], pick_g)).astype(BF16)
         wq[2 * m + 1] = (dot(slab[4 * m + 1], pick_k) + dot(slab[4 * m + 2], pick_v)).astype(BF16)
 
-    some_bulk(15 - EARLY)
+    some_bulk(2)
     for cp in ld_pool:
         cp.wait()
     want = (iota((QT, 128), 0) + QT * k).astype(F32)
@@ -416,7 +455,7 @@
             lane < 64, own_kv[0:48, 128:256], pltpu.roll(own_kv[48:96, 128:256], 64, 1)
         ).astype(BF16)
         kv[b, mine, 2] = own_kv[48:96, 0:128].astype(BF16)
-        for j in range(1, NR):
+        for j in FAR_FIRST:
             cp = rcopy(
                 kv_slot(b, mine),
                 kv_slot(b, mine),
@@ -434,13 +473,14 @@
             )
         fwd[0].start()
         pend += fwd
+        some_bulk(3 if b == 0 else 8)
         qg = dot(n, wq[2 * b])
         q = qg[:, 0:128].astype(BF16).astype(F32)
         gate = jax.nn.sigmoid(qg[:, 128:256])
         qs = jnp.concatenate([jnp.where(lq < 48, q, 0.0), jnp.where(lq < 48, 0.0, q)], 0).astype(
             BF16
         )
-        for j in range(1, NR):
+        for j in reversed(FAR_FIRST):
             s = 2 * ((r + j) % NR) + k
             rcopy(kv_slot(b, s), kv_slot(b, s), kv_ss.at[b, 0], kv_rs.at[b, s], sib).wait_recv()
             fwd[j].start()
@@ -449,17 +489,22 @@
             s = (c + j) % NC
             rcopy(bb.at[b, s], bb.at[b, s], b_ss.at[b, 0], b_rs.at[b, s], sib).wait_recv()
 
+        sizes = jnp.concatenate([bb[b, s, 72:ZR, :] for s in range(NC)], 0).astype(F32)
+        steps = jnp.transpose(sizes * (1.0 / (32767.0 * 65536.0)))
+
         def scores(slots, mx):
             keys = []
             for s in slots:
                 keys += [kv[b, s, 0], kv[b, s, 2], pad]
             dots = dot_t(qs, jnp.concatenate(keys, 0)) * (1.0 / math.sqrt(48.0))
             for d, slot in enumerate(slots):
-                first = (QT * slot).astype(F32)
-                ok = lanef + first < jnp.minimum(nvalid, first + QT)
+                ok = lanef + QT * slot < jnp.minimum(nvalid, QT * slot + QT)
+                word = bb[b, slot, 0:72, :]
+                both = (lax.shift_right_logical(word, 16), word & 65535)
                 parts = []
                 for h in range(2):
-                    m = bb[b, slot, h]
+                    step = steps[0:72, 8 * slot + h : 8 * slot + h + 1]
+                    m = (both[h].astype(F32) - 32768.0) * step
                     tail = jnp.where(
                         lane < 32,
                         pltpu.roll(m[0:24], 32, 1),
@@ -471,53 +516,42 @@
                 sc = dots[:, 128 * d : 128 * d + 128] + jnp.concatenate(parts, 0)
                 sc = jnp.where(ok, sc, NEG)
                 ssc[slot] = sc
+                mid = kv[b, slot, 1]
+                vb[slot, 0:48, 0:128] = kv[b, slot, 0]
+                vb[slot, 0:48, 128:256] = mid * left
+                vb[slot, 48:96, 0:128] = kv[b, slot, 2]
+                vb[slot, 48:96, 128:256] = mid * right
                 mx = jnp.maximum(mx, sc)
             return mx
 
         mx = jnp.full((2 * QT, 128), 2 * NEG, F32)
         if b == 0:
-            some_bulk(G0)
+            some_bulk(4)
         for grp in range(4):
-            slots = []
-            for j in (2 * grp, 2 * grp + 1):
-                s = 2 * ((r + j) % NR) + k
-                slots.append(s)
-            for j in (2 * grp, 2 * grp + 1):
-                s = 2 * ((r + j) % NR) + 1 - k
-                slots.append(s)
+            for row in (2 * grp, 2 * grp + 1):
+                s = 2 * row + 1 - k
                 rcopy(kv_slot(b, s), kv_slot(b, s), kv_ss.at[b, 0], kv_rs.at[b, s], sib).wait_recv()
+            slots = [4 * grp + d for d in range(4)]
             mx = scores(slots, mx)
         top = jnp.max(mx, -1, keepdims=True)
-
-        def value_step(s4, state):
-            tot, o = state
-            ps = []
-            vals = []
-            for d in range(4):
-                s = 4 * s4 + d
-                e = jnp.exp(ssc[s] - top)
-                tot = tot + e
-                ps.append(e.astype(BF16))
-                mid = kv[b, s, 1]
-                vals.append(jnp.concatenate([kv[b, s, 0], mid * left], 1))
-                vals.append(jnp.concatenate([kv[b, s, 2], mid * right], 1))
-                vals.append(jnp.concatenate([pad, pad], 1))
-            return tot, o + dot(jnp.concatenate(ps, 1), jnp.concatenate(vals, 0))
-
-        tot, o = lax.fori_loop(
-            0, 4, value_step, (jnp.zeros((2 * QT, 128), F32), jnp.zeros((2 * QT, 256), F32))
-        )
+        tot = jnp.zeros((2 * QT, 128), F32)
+        ps = []
+        for s in range(NC):
+            e = jnp.exp(ssc[s] - top)
+            tot = tot + e
+            ps.append(e.astype(BF16))
+        o = dot(jnp.concatenate(ps, 1), vb[...].reshape(NC * 128, 256))
         inv = 1.0 / jnp.sum(tot, -1, keepdims=True)
         o_a = o[:QT, 0:128] * inv[:QT]
         o_b = (o[:, 128:256] + pltpu.roll(o[:, 128:256], 64, 1)) * inv
         o = jnp.where(lq < 16, o_b[:QT], jnp.where(lq < 64, o_b[QT:], jnp.where(lq < 96, 0.0, o_a)))
         ob[b, i] = (gate * o).astype(BF16)
-        for j in range(1, NCH):
+        for j in FAR_FIRST:
             cp = rcopy(ob.at[b, i], ob.at[b, i], o_ss.at[b, j], o_rs.at[b, i], chip(j))
             cp.start()
             pend.append(cp)
         if b == 0:
-            some_bulk(G1)
+            some_bulk(5)
             for cp in ld_tok:
                 cp.wait()
             for cp in swap:
@@ -526,30 +560,31 @@
             s = (i + j) % NCH
             rcopy(ob.at[b, s], ob.at[b, s], o_ss.at[b, 0], o_rs.at[b, s], sib).wait_recv()
         gated = jnp.concatenate([ob[b, s] for s in range(NCH)], 1)
-        act[...] += dot(gated, topad[8 * b : 8 * b + 8].reshape(1024, 768))
-
-        m = normed(act[...]).astype(BF16)
+        mid_act = act[...] + dot(gated, topad[8 * b : 8 * b + 8].reshape(1024, 768))
+        act[...] = mid_act
+
+        m = normed(mid_act).astype(BF16)
         swish = jax.nn.silu(dot_t(m, tin[b, 0]))
         hidden = (swish * dot_t(m, tin[b, 1])).astype(BF16)
         prt[b] = dot(hidden, tout[b]).astype(BF16)
-        for o_ in range(OWN):
-
-            @pl.when(i != o_)
+        for u in range(OWN):
+
+            @pl.when(unit != u)
             def _():
                 rcopy(
-                    prt.at[b, 16 * o_ : 16 * o_ + 16],
+                    prt.at[b, 16 * u : 16 * u + 16],
                     rsb.at[b, i],
-                    r_ss.at[b, o_],
+                    r_ss.at[b, u],
                     r_rs.at[b, i],
-                    (r, 2 * o_ + k),
+                    owner_dev(u),
                 ).start()
 
         if b == 0:
-            some_bulk(G2)
+            some_bulk(6)
 
         @pl.when(is_owner)
         def _():
-            row0 = pl.multiple_of(16 * i, 16)
+            row0 = pl.multiple_of(16 * unit, 16)
             rsb[b, i] = prt[b, pl.ds(row0, 16), :]
             for j in range(1, NCH):
                 s = (i + j) % NCH
@@ -558,28 +593,30 @@
             for s in range(1, NCH):
                 total = total + rsb[b, s].astype(F32)
             if b == 0:
-                db[i] = total.astype(BF16)
-                for j in range(1, NCH):
-                    rcopy(db.at[i], db.at[i], d_ss.at[j], d_rs.at[i], chip(j)).start()
+                db[unit] = total.astype(BF16)
+                for j in FAR_FIRST:
+                    rcopy(
+                        db.at[unit], db.at[unit], d_ss.at[j], d_rs.at[unit], chip(j)
+                    ).start()
             else:
                 last = act[pl.ds(row0, 16), :] + total
-                here = pl.multiple_of(64 + QT * k + 16 * i, 16)
+                here = pl.multiple_of(64 + QT * k + 16 * unit, 16)
                 mine_p = proj.at[pl.ds(here, 16)]
                 proj[pl.ds(here, 16), :] = dot(
                     normed(last).astype(BF16), tok_atom[...]
                 ).astype(BF16)
                 for j in range(1, NC):
                     rcopy(
-                        mine_p, mine_p, p_ss.at[j], p_rs.at[OWN * k + i], (r, (c + j) % NC)
+                        mine_p, mine_p, p_ss.at[j], p_rs.at[OWN * k + unit], (r, (c + j) % NC)
                     ).start()
 
                 @pl.when(is_tail)
                 def _():
                     rcopy(
                         mine_p,
-                        proj.at[pl.ds(pl.multiple_of(16 * (i - 2), 16), 16)],
+                        proj.at[pl.ds(pl.multiple_of(16 * (unit - 2), 16), 16)],
                         p_ss.at[16],
-                        p_rs.at[10 + i],
+                        p_rs.at[10 + unit],
                         ((r + 1) % NR, 0),
                     ).start()
 
@@ -587,17 +624,17 @@
                 def _():
                     rcopy(
                         mine_p,
-                        proj.at[pl.ds(pl.multiple_of(256 + 16 * i, 16), 16)],
+                        proj.at[pl.ds(pl.multiple_of(256 + 16 * unit, 16), 16)],
                         p_ss.at[16],
-                        p_rs.at[12 + i],
+                        p_rs.at[12 + unit],
                         ((r + NR - 1) % NR, NC - 1),
                     ).start()
 
         if b == 0:
-            some_bulk(15)
+            some_bulk(7)
             for o_ in range(OWN):
 
-                @pl.when(i != o_)
+                @pl.when(unit != o_)
                 def _():
                     rcopy(db.at[o_], db.at[o_], d_ss.at[0], d_rs.at[o_], sib).wait_recv()
 
@@ -628,7 +665,7 @@
 
     for s in range(2 * OWN):
 
-        @pl.when(jnp.logical_or(i >= OWN, s != OWN * k + i))
+        @pl.when(jnp.logical_or(jnp.logical_not(is_owner), s != OWN * k + unit))
         def _():
             proj_wait(s, 64 + 16 * s, 16)
 
@@ -648,12 +685,12 @@
     n3 = normed(x3.astype(F32)).astype(BF16)
     out[...] = dot_t(pos[...], n3)
 
-    for cp in halo + swap + edge + x_send + x_fwd + b_send[0] + b_send[1] + pend:
+    for cp in halo + swap + edge + x_send + x_fwd + b_sent + pend:
         cp.wait_send()
     for b in range(2):
         for o_ in range(OWN):
 
-            @pl.when(i != o_)
+            @pl.when(unit != o_)
             def _():
                 src = prt.at[b, 16 * o_ : 16 * o_ + 16]
                 rcopy(src, rsb.at[b, i], r_ss.at[b, o_], r_rs.at[b, i], sib).wait_send()
@@ -661,8 +698,8 @@
     @pl.when(is_owner)
     def _():
         for j in range(1, NCH):
-            rcopy(db.at[i], db.at[i], d_ss.at[j], d_rs.at[i], sib).wait_send()
-        ref = proj.at[pl.ds(pl.multiple_of(64 + QT * k + 16 * i, 16), 16)]
+            rcopy(db.at[0], db.at[0], d_ss.at[j], d_rs.at[0], sib).wait_send()
+        ref = proj.at[pl.ds(pl.multiple_of(64 + QT * k + 16 * unit, 16), 16)]
         for j in range(1, NC):
             rcopy(ref, ref, p_ss.at[j], p_rs.at[0], sib).wait_send()
 
@@ -714,10 +751,11 @@
         V((2, 64, 128), BF16),
         V((16, 160, 128), BF16),
         V((2, 80, 128), BF16),
-        V((32, 144, 128), F32),
-        V((2, 16, 2, 72, 128), F32),
+        V((16, 2, ZR, 128), jnp.int32),
+        V((2, 16, ZR, 128), jnp.int32),
         V((2, 16, 3, 48, 128), BF16),
         V((16, 192, 128), F32),
+        V((16, 128, 256), BF16),
         V((2, 8, QT, 128), BF16),
         V((2, QT, 768), BF16),
         V((2, 8, 16, 768), BF16),

time: 92 us -> 85.2 us (0.926)
  Pallas kernels: 90.6 us -> 83.8 us
    pallas_call x1, Pallas kernels: 90.6 us -> 83.8 us  [body(): pl.pallas_call(kernel, out_shape=jax.ShapeDtypeStruct((3, 128), F32), in_...]
where the time goes in v4:
time: 85.2 us; the launch traced here: 85 us
  Pallas kernels  83.8 us (98%)
  local copies, waits for them, and re-layouts  1.26 us (1%)
    pallas_call x1, Pallas kernels, body(): pl.pallas_call(kernel, out_shape=jax.ShapeDtypeStruct((3, 128), F32), in_...  83.8 us

profile of v4, /device:TPU:1, one launch (start us, length us, event | category | flops | bytes accessed | tf_op | source)
XLA Modules:
  0.0 85.0 jit_solution(6677124559574634231)
XLA Ops:
  0.0 83.8 %diffusion_step.1 = f32[3,128]{1,0:T(4,128)} custom-call(s32[4]{0:T(128)} %ws.1, s32[1,128]{1,0:T(1,128)} %bitcast.13, s32[12,128]{1,0:T(8,128)} %bitcast.11, bf16[128,128]{1,0:T(8,128)(2,1)} %x_in.1, bf16[32,128]{1,0:T(8,128)(2,1)} %bitcast.12, bf16[192,768]{1,0:T(8,128)(2,1)} %cond_h.1, bf16[192,96,128]{2,1,0:T(8,128)(2,1)} %pair_h.1, ...), custom_call_target="tpu_custom_call" | custom-call | tf_op jit(solution)/shard_map/diffusion_step/pallas_call | solution.py:789
  83.8 1.3 %copy.20 = f32[3,128]{1,0:T(4,128)} copy(f32[3,128]{1,0:T(4,128)} %diffusion_step.1) | data formatting | bytes 3072

commit v5 on v4

--- a/solution.py
+++ b/solution.py
@@ -19,16 +19,17 @@
 CHIP_OF = (0, 3, 6, 5, 2, 1)
 QT = 96
 BULK = (
-    ((0, 2, 0), (0, 6, 0), (0, 4, 0), (0, 1, 0), (0, 7, 0), (0, 3, 0)),
+    ((0, 2, 0), (0, 6, 0), (0, 4, 0), (0, 1, 0), (0, 7, 0), (0, 3, 0), (0, 5, 0)),
     (),
-    ((0, 5, 0), (0, 2, 1), (0, 6, 1), (0, 4, 1), (0, 1, 1), (0, 7, 1), (0, 3, 1), (0, 5, 1), (0, 0, 0)),
+    ((0, 2, 1), (0, 6, 1), (0, 4, 1), (0, 1, 1), (0, 7, 1), (0, 3, 1), (0, 5, 1), (0, 0, 0)),
     ((1, 2, 0), (1, 6, 0), (1, 4, 0)),
-    ((1, 1, 0), (1, 1, 1), (1, 4, 1)),
+    ((1, 2, 1), (1, 6, 1), (1, 4, 1), (1, 1, 0), (1, 1, 1)),
     ((1, 7, 0), (1, 7, 1)),
     ((1, 3, 0), (1, 3, 1)),
-    ((1, 5, 0), (1, 5, 1)),
-    ((1, 2, 1), (1, 6, 1), (1, 0, 0)),
+    ((1, 5, 0), (1, 5, 1), (1, 0, 0)),
+    (),
 )
+PRE, POST = (0, 1), (2,)
 ZR = 80
 BT = 8
 
@@ -119,8 +120,6 @@
     rsb,
     db,
     act,
-    feats,
-    hots,
     proj,
     lsem,
     h_ss,
@@ -218,15 +217,14 @@
     lane32 = iota((32, 128), 1)
     zf = zb.reshape(16 * 2 * ZR, 128)
 
-    def bias_half(kp):
+    def bias_part(kp, parts, sizes):
         def words(u, first):
             return lax.shift_left(u[first : first + 8], 16) | u[first + 8 : first + 16]
 
         def put(b, row, value):
             zf[pl.ds(b * 16 * ZR + kp * ZR + row, 8, stride=2 * ZR), :] = value
 
-        sizes = jnp.zeros((32, 128), jnp.int32)
-        for kb in range(3):
+        for kb in parts:
 
             def tiles(n, sizes):
                 t = 24 * kb + BT * n
@@ -247,6 +245,8 @@
                 return sizes
 
             sizes = lax.fori_loop(0, 24 // BT, tiles, sizes)
+        if 2 not in parts:
+            return sizes
         for b in range(2):
             for odd in range(2):
                 put(b, 72 + odd, sizes[16 * b + 8 * odd : 16 * b + 8 * odd + 8])
@@ -275,7 +275,8 @@
 
     ld_pair[0].wait()
     ld_pair[1].wait()
-    bias_half(0)
+    no_sizes = jnp.zeros((32, 128), jnp.int32)
+    sizes = bias_part(0, PRE, no_sizes)
     extra = jnp.where(jnp.logical_or(is_tail, is_head), 1, 0)
     pl.semaphore_wait(bar, 24 + extra)
 
@@ -311,17 +312,8 @@
             b_sent.append(bias_sib(b) if j == 0 else bias_send(b, j, core))
             b_sent[-1].start()
 
+    bias_part(0, POST, sizes)
     some_bulk(0)
-    ld_pair[2].wait()
-    ld_pair[3].wait()
-    bias_half(1)
-    b_own = []
-    for b in range(2):
-        cp = pltpu.make_async_copy(bias_src(b, i, k), bb.at[b, c], lsem.at[nload[0] + b])
-        cp.start()
-        b_own.append(cp)
-
-    some_bulk(1)
     for cp in ld_enc:
         cp.wait()
     for cp in halo:
@@ -371,6 +363,16 @@
     for cp in edge:
         cp.start()
 
+    ld_pair[2].wait()
+    ld_pair[3].wait()
+    bias_part(1, (0, 1, 2), no_sizes)
+    b_own = []
+    for b in range(2):
+        cp = pltpu.make_async_copy(bias_src(b, i, k), bb.at[b, c], lsem.at[nload[0] + b])
+        cp.start()
+        b_own.append(cp)
+
+
     for cp in ld_slab:
         cp.wait()
     e_row = iota((256, 256), 0) - shift
@@ -388,47 +390,42 @@
     pick_k = onehot(picker(0, 96, 0))
     pick_v = onehot(picker(96, 192, 0))
 
+    some_bulk(2)
     @pl.loop(0, 2)
     def _(m):
         wq[2 * m] = (dot(slab[4 * m], pick_q) + dot(slab[4 * m + 3], pick_g)).astype(BF16)
         wq[2 * m + 1] = (dot(slab[4 * m + 1], pick_k) + dot(slab[4 * m + 2], pick_v)).astype(BF16)
 
-    some_bulk(2)
     for cp in ld_pool:
         cp.wait()
     want = (iota((QT, 128), 0) + QT * k).astype(F32)
 
-    def pool_slot(s, n):
-        feats[n] = jnp.maximum(dot(x1all[s, 16:144, :], pool[...]), 0.0).astype(BF16)
-        t = x1all[s, 0:16, :].astype(F32)[0:1]
-        hots[n] = jnp.where(t == want, 1.0, 0.0).astype(BF16)
-
-    def pool_group(g):
-        hot = jnp.concatenate([hots[4 * g + d] for d in range(4)], 1)
-        part = dot(hot, feats[4 * g : 4 * g + 4].reshape(512, 768))
-        n = hot[:, 0:128].astype(F32)
-        for d in range(1, 4):
-            n = n + hot[:, 128 * d : 128 * d + 128].astype(F32)
-        if g == 0:
-            act[...] = part
-        else:
-            act[...] += part
+    def pool_group(slots, first):
+        xs = jnp.concatenate([x1all[s, 16:144, :] for s in slots], 0)
+        feats = jnp.maximum(dot(xs, pool[...]), 0.0).astype(BF16)
+        hots = []
+        n = jnp.zeros((QT, 128), F32)
+        for s in slots:
+            t = x1all[s, 0:16, :].astype(F32)[0:1]
+            hots.append(jnp.where(t == want, 1.0, 0.0))
+            n = n + hots[-1]
+        part = dot(jnp.concatenate(hots, 1).astype(BF16), feats)
+        act[...] = part if first else act[...] + part
         return n
 
+    near4, far4 = (0, 2, 6, 1), (7, 4, 3, 5)
     cnt = jnp.zeros((QT, 128), F32)
-    for j in range(NCH):
-        s = 2 * ((i + j) % NCH) + k
-        if j > 0:
-            rcopy(x1_slot(s), x1_slot(s), x_ss.at[0], x_rs.at[s], sib).wait_recv()
-            x_fwd[j].start()
-        pool_slot(s, j)
-        if j % 4 == 3:
-            cnt = cnt + pool_group(j // 4)
-    for j in range(NCH):
-        x_far[j].wait_recv()
-        pool_slot(2 * ((i + j) % NCH) + 1 - k, NCH + j)
-        if j % 4 == 3:
-            cnt = cnt + pool_group(2 + j // 4)
+    for quad in (near4, far4):
+        for j in quad:
+            s = 2 * ((i + j) % NCH) + k
+            if j > 0:
+                rcopy(x1_slot(s), x1_slot(s), x_ss.at[0], x_rs.at[s], sib).wait_recv()
+                x_fwd[j].start()
+        cnt = cnt + pool_group([2 * ((i + j) % NCH) + k for j in quad], quad == near4)
+    for quad in (near4, far4):
+        for j in quad:
+            x_far[j].wait_recv()
+        cnt = cnt + pool_group([2 * ((i + j) % NCH) + 1 - k for j in quad], False)
     act[...] = act[...] / jnp.sum(cnt, -1, keepdims=True) + cond[...].astype(F32)
 
     nvalid = jnp.sum(
@@ -492,18 +489,19 @@
         sizes = jnp.concatenate([bb[b, s, 72:ZR, :] for s in range(NC)], 0).astype(F32)
         steps = jnp.transpose(sizes * (1.0 / (32767.0 * 65536.0)))
 
-        def scores(slots, mx):
+        def scores(slots, steps, mx):
             keys = []
             for s in slots:
                 keys += [kv[b, s, 0], kv[b, s, 2], pad]
             dots = dot_t(qs, jnp.concatenate(keys, 0)) * (1.0 / math.sqrt(48.0))
             for d, slot in enumerate(slots):
-                ok = lanef + QT * slot < jnp.minimum(nvalid, QT * slot + QT)
+                first = (QT * slot).astype(F32)
+                ok = lanef + first < jnp.minimum(nvalid, first + QT)
                 word = bb[b, slot, 0:72, :]
                 both = (lax.shift_right_logical(word, 16), word & 65535)
                 parts = []
                 for h in range(2):
-                    step = steps[0:72, 8 * slot + h : 8 * slot + h + 1]
+                    step = steps[:, 8 * d + h : 8 * d + h + 1]
                     m = (both[h].astype(F32) - 32768.0) * step
                     tail = jnp.where(
                         lane < 32,
@@ -527,12 +525,14 @@
         mx = jnp.full((2 * QT, 128), 2 * NEG, F32)
         if b == 0:
             some_bulk(4)
-        for grp in range(4):
-            for row in (2 * grp, 2 * grp + 1):
+        for turn in (0, 1, 3, 2):
+            z = (r // 2 + turn) % 4
+            for row in (2 * z, 2 * z + 1):
                 s = 2 * row + 1 - k
                 rcopy(kv_slot(b, s), kv_slot(b, s), kv_ss.at[b, 0], kv_rs.at[b, s], sib).wait_recv()
-            slots = [4 * grp + d for d in range(4)]
-            mx = scores(slots, mx)
+            slots = [4 * z + d for d in range(4)]
+            near_steps = pltpu.roll(steps[0:72], (128 - 32 * z) % 128, 1)
+            mx = scores(slots, near_steps, mx)
         top = jnp.max(mx, -1, keepdims=True)
         tot = jnp.zeros((2 * QT, 128), F32)
         ps = []
@@ -761,8 +761,6 @@
         V((2, 8, 16, 768), BF16),
         V((6, 16, 768), BF16),
         V((QT, 768), F32),
-        V((16, 128, 768), BF16),
-        V((16, QT, 128), BF16),
         V((384, 128), BF16),
         dma((24,)),
         dma((2,)),

time: 85.2 us -> 83.4 us (0.979)
  Pallas kernels: 83.8 us -> 81.9 us
    pallas_call x1, Pallas kernels: 83.8 us -> 81.9 us  [body(): pl.pallas_call(kernel, out_shape=jax.ShapeDtypeStruct((3, 128), F32), in_...]
where the time goes in v5:
time: 83.4 us; the launch traced here: 83.2 us
  Pallas kernels  81.9 us (98%)
  local copies, waits for them, and re-layouts  1.26 us (2%)
    pallas_call x1, Pallas kernels, body(): pl.pallas_call(kernel, out_shape=jax.ShapeDtypeStruct((3, 128), F32), in_...  81.9 us

profile of v5, /device:TPU:1, one launch (start us, length us, event | category | flops | bytes accessed | tf_op | source)
XLA Modules:
  0.0 83.2 jit_solution(10074998859490468240)
XLA Ops:
  0.0 81.9 %diffusion_step.1 = f32[3,128]{1,0:T(4,128)} custom-call(s32[4]{0:T(128)} %ws.1, s32[1,128]{1,0:T(1,128)} %bitcast.13, s32[12,128]{1,0:T(8,128)} %bitcast.11, bf16[128,128]{1,0:T(8,128)(2,1)} %x_in.1, bf16[32,128]{1,0:T(8,128)(2,1)} %bitcast.12, bf16[192,768]{1,0:T(8,128)(2,1)} %cond_h.1, bf16[192,96,128]{2,1,0:T(8,128)(2,1)} %pair_h.1, ...), custom_call_target="tpu_custom_call" | custom-call | tf_op jit(solution)/shard_map/diffusion_step/pallas_call | solution.py:787
  81.9 1.3 %copy.20 = f32[3,128]{1,0:T(4,128)} copy(f32[3,128]{1,0:T(4,128)} %diffusion_step.1) | data formatting | bytes 3072

commit v6 on v5

--- a/solution.py
+++ b/solution.py
@@ -173,6 +173,30 @@
             src_ref=src, dst_ref=dst, send_sem=ss, recv_sem=rs, device_id=dev, device_id_type=MESH
         )
 
+    proj[...] = jnp.zeros((384, 128), BF16)
+
+    bar = pltpu.get_barrier_semaphore()
+
+    def greet(dev):
+        pl.semaphore_signal(bar, inc=1, device_id=dev, device_id_type=MESH)
+
+    for j in range(1, NC):
+        greet((r, (c + j) % NC))
+    for j in range(1, NR):
+        greet(((r + j) % NR, c))
+    greet(nxt)
+    greet(prv)
+
+    @pl.when(c == 0)
+    def _():
+        for u in range(2, OWN):
+            greet(((r + NR - 1) % NR, 2 * ((CHIP_OF[u] + 4) % NCH) + 1))
+
+    @pl.when(c == NC - 1)
+    def _():
+        for u in range(4):
+            greet(((r + 1) % NR, 2 * CHIP_OF[u]))
+
     nload = [0]
 
     def load(src, dst):
@@ -208,7 +232,6 @@
     zb[:, :, 72:, :] = jnp.zeros((16, 2, 8, 128), jnp.int32)
     vb[:, 96:128, :] = jnp.zeros((16, 32, 256), BF16)
     topad[:, 64:96, :] = jnp.zeros((16, 32, 768), BF16)
-    proj[...] = jnp.zeros((384, 128), BF16)
 
     order = iota((32, 32), 1) == 16 * (iota((32, 32), 0) // 16) + 2 * (iota((32, 32), 0) % 8) + (
         iota((32, 32), 0) // 8
@@ -250,28 +273,6 @@
         for b in range(2):
             for odd in range(2):
                 put(b, 72 + odd, sizes[16 * b + 8 * odd : 16 * b + 8 * odd + 8])
-
-    bar = pltpu.get_barrier_semaphore()
-
-    def greet(dev):
-        pl.semaphore_signal(bar, inc=1, device_id=dev, device_id_type=MESH)
-
-    for j in range(1, NC):
-        greet((r, (c + j) % NC))
-    for j in range(1, NR):
-        greet(((r + j) % NR, c))
-    greet(nxt)
-    greet(prv)
-
-    @pl.when(c == 0)
-    def _():
-        for u in range(2, OWN):
-            greet(((r + NR - 1) % NR, 2 * ((CHIP_OF[u] + 4) % NCH) + 1))
-
-    @pl.when(c == NC - 1)
-    def _():
-        for u in range(4):
-            greet(((r + 1) % NR, 2 * CHIP_OF[u]))
 
     ld_pair[0].wait()
     ld_pair[1].wait()
@@ -556,11 +557,17 @@
                 cp.wait()
             for cp in swap:
                 cp.wait_recv()
-        for j in range(1, NCH):
-            s = (i + j) % NCH
-            rcopy(ob.at[b, s], ob.at[b, s], o_ss.at[b, 0], o_rs.at[b, s], sib).wait_recv()
-        gated = jnp.concatenate([ob[b, s] for s in range(NCH)], 1)
-        mid_act = act[...] + dot(gated, topad[8 * b : 8 * b + 8].reshape(1024, 768))
+        mid_act = act[...]
+        for quad in (near4, far4):
+            gated = []
+            weights = []
+            for j in quad:
+                s = (i + j) % NCH
+                if j > 0:
+                    rcopy(ob.at[b, s], ob.at[b, s], o_ss.at[b, 0], o_rs.at[b, s], sib).wait_recv()
+                gated.append(ob[b, s])
+                weights.append(topad[8 * b + s])
+            mid_act = mid_act + dot(jnp.concatenate(gated, 1), jnp.concatenate(weights, 0))
         act[...] = mid_act
 
         m = normed(mid_act).astype(BF16)
@@ -663,6 +670,16 @@
         ref = proj.at[row : row + n]
         rcopy(ref, ref, p_ss.at[0], p_rs.at[slot], sib).wait_recv()
 
+    for cp in halo + swap + edge + x_send + x_fwd + b_sent + pend:
+        cp.wait_send()
+    for b in range(2):
+        for o_ in range(OWN):
+
+            @pl.when(unit != o_)
+            def _():
+                src = prt.at[b, 16 * o_ : 16 * o_ + 16]
+                rcopy(src, rsb.at[b, i], r_ss.at[b, o_], r_rs.at[b, i], sib).wait_send()
+
     for s in range(2 * OWN):
 
         @pl.when(jnp.logical_or(jnp.logical_not(is_owner), s != OWN * k + unit))
@@ -684,16 +701,6 @@
     x3 = atom_layer(x2, valid, dec_in, dec_out)
     n3 = normed(x3.astype(F32)).astype(BF16)
     out[...] = dot_t(pos[...], n3)
-
-    for cp in halo + swap + edge + x_send + x_fwd + b_sent + pend:
-        cp.wait_send()
-    for b in range(2):
-        for o_ in range(OWN):
-
-            @pl.when(unit != o_)
-            def _():
-                src = prt.at[b, 16 * o_ : 16 * o_ + 16]
-                rcopy(src, rsb.at[b, i], r_ss.at[b, o_], r_rs.at[b, i], sib).wait_send()
 
     @pl.when(is_owner)
     def _():

time: 83.4 us -> 83.9 us (level)
  no operation moved by 1% of the time
where the time goes in v6:
time: 83.9 us; the launch traced here: 83.7 us
  Pallas kernels  82.4 us (98%)
  local copies, waits for them, and re-layouts  1.26 us (2%)
    pallas_call x1, Pallas kernels, body(): pl.pallas_call(kernel, out_shape=jax.ShapeDtypeStruct((3, 128), F32), in_...  82.4 us

profile of v6, /device:TPU:1, one launch (start us, length us, event | category | flops | bytes accessed | tf_op | source)
XLA Modules:
  0.0 83.7 jit_solution(7949570573492084434)
XLA Ops:
  0.0 82.4 %diffusion_step.1 = f32[3,128]{1,0:T(4,128)} custom-call(s32[4]{0:T(128)} %ws.1, s32[1,128]{1,0:T(1,128)} %bitcast.13, s32[12,128]{1,0:T(8,128)} %bitcast.11, bf16[128,128]{1,0:T(8,128)(2,1)} %x_in.1, bf16[32,128]{1,0:T(8,128)(2,1)} %bitcast.12, bf16[192,768]{1,0:T(8,128)(2,1)} %cond_h.1, bf16[192,96,128]{2,1,0:T(8,128)(2,1)} %pair_h.1, ...), custom_call_target="tpu_custom_call" | custom-call | tf_op jit(solution)/shard_map/diffusion_step/pallas_call | solution.py:794
  82.4 1.3 %copy.20 = f32[3,128]{1,0:T(4,128)} copy(f32[3,128]{1,0:T(4,128)} %diffusion_step.1) | data formatting | bytes 3072
